TPU v7x, 128 devices: a whole 4x4x4 slice. The times are simulated.
128 devices in a mesh: section: 4 (over x_lo, core), expert: 32 (over z, y, x_hi).
Axes of the slice: x: 4 (x_hi: 2, x_lo: 2; x = x_hi * 2 + x_lo), y: 4, z: 4, core: 2. Of those that a mesh axis runs over, the one named last changes fastest.
Arguments:
- fwd_in: bfloat16 [4, 2048, 7168], P('section', 'expert'), may hold values from -6 to 6
- gains: float32 [4, 7168], P('section'), may hold values from 0.25 to 1.75
- gate_weight: bfloat16 [4, 7168, 8192], P('section', None, 'expert'), may hold values from -0.0625 to 0.0625
- up_weight: bfloat16 [4, 7168, 8192], P('section', None, 'expert'), may hold values from -0.0625 to 0.0625
- down_weight: bfloat16 [4, 8192, 7168], P('section', 'expert'), may hold values from -0.1875 to 0.1875
- fwd_routes: int32 [4, 2048, 2], P('section', 'expert'), may hold values from 0 to 7, all different within a row; in each aligned block of 64 rows (0 to 63, 64 to 127, ..., all dimensions but the last counted through in order) at most 20 rows name the same one
- fwd_probs: float32 [4, 2048, 2], P('section', 'expert'), may hold values from 0.1 to 1
- bwd_grad: bfloat16 [4, 2048, 7168], P('section', 'expert'), may hold values from -6 to 6
- bwd_input: bfloat16 [4, 2048, 7168], P('section', 'expert'), may hold values from -6 to 6
- bwd_routes: int32 [4, 2048, 2], P('section', 'expert'), may hold values from 0 to 7, all different within a row; in each aligned block of 64 rows (0 to 63, 64 to 127, ..., all dimensions but the last counted through in order) at most 20 rows name the same one
- bwd_probs: float32 [4, 2048, 2], P('section', 'expert'), may hold values from 0.1 to 1
- bwd_stash: bfloat16 [4, 20480, 512], P('section', 'expert'), may hold values from -6 to 6
Outputs:
- fwd_out: bfloat16 [4, 2048, 7168], P('section', 'expert')
- bwd_out: bfloat16 [4, 2048, 7168], P('section', 'expert')
Inputs may be any that keep to these rules, and one draw needn't show every extreme that they name: `fwd_routes`: each row names 2 different experts; in the rows of one device no expert is named by more than 20 rows, and in every draw some expert is named by exactly 20 rows of some device. `bwd_routes`: each row names 2 different experts; in the rows of one device no expert is named by more than 20 rows, and in every draw some expert is named by exactly 20 rows of some device.
All inputs are finite; a program needn't handle non-finite values.
Results may differ from a plain program's by a relative error of at most 0.0048.
Values may be sent and summed in bfloat16 or wider, within the bound.
A program may use at most 192 MiB of HBM per device.

v0:
```python
import jax
import jax.numpy as jnp
from jax import lax
from jax.sharding import PartitionSpec as P

SPLIT = 4


EPSILON = 1e-06


def passed_along(block, axis, distance):
    devices = range(lax.axis_size(axis))
    route = [((i - distance) % len(devices), i) for i in devices]
    return lax.ppermute(block, axis, route)


def rms_scale(hidden_state, norm_gain):
    return (
        hidden_state
        * lax.rsqrt(jnp.mean(hidden_state * hidden_state, axis=-1, keepdims=True) + EPSILON)
        * norm_gain
    )


def slot_layout(routes, experts, capacity, row_block):
    token_count, top_count = routes.shape
    expert_ids = routes.reshape(token_count * top_count)
    onehot = (expert_ids[:, None] == jnp.arange(experts, dtype=jnp.int32)[None, :]).astype(
        jnp.int32
    )
    before = jnp.cumsum(onehot, axis=0) - onehot
    position = jnp.sum(before * onehot, axis=1)
    slot_index = expert_ids * capacity + position
    matches = jnp.arange(experts * capacity, dtype=jnp.int32)[:, None] == slot_index[None, :]
    token_match = jnp.any(
        matches.reshape(experts * capacity, token_count, top_count), axis=2
    ).astype(jnp.bfloat16)
    buffer = jnp.dot(token_match, row_block, preferred_element_type=jnp.float32).astype(
        jnp.bfloat16
    )
    return (buffer, slot_index)


def dispatch(buffer, experts, capacity):
    feature = buffer.shape[1]
    copies = jnp.broadcast_to(
        buffer.reshape(experts, 1, capacity, feature), (experts, SPLIT, capacity, feature)
    )
    return lax.all_to_all(
        copies.reshape(experts * SPLIT * capacity, feature),
        "expert",
        split_axis=0,
        concat_axis=0,
        tiled=True,
    )


def send_back(partial_rows, experts, capacity):
    feature = partial_rows.shape[1]
    shaped = partial_rows.reshape(1, experts * SPLIT * capacity, feature)
    returned = lax.all_to_all(shaped, "expert", split_axis=1, concat_axis=1, tiled=True)
    summed = jnp.sum(
        returned.reshape(experts, SPLIT, capacity, feature).astype(jnp.float32), axis=1
    )
    return summed.reshape(experts * capacity, feature)


def combine_rows(totals, result_index, probs):
    token_count, top_count = probs.shape
    picked = totals[result_index].reshape(token_count, top_count, totals.shape[1])
    return jnp.sum(picked * probs[:, :, None], axis=1)


def expert_forward(row_block, gate_part, up_part, down_part):
    gate = jnp.dot(row_block, gate_part, preferred_element_type=jnp.float32)
    upper = jnp.dot(row_block, up_part, preferred_element_type=jnp.float32)
    hidden = (jax.nn.silu(gate) * upper).astype(jnp.bfloat16)
    return jnp.dot(hidden, down_part, preferred_element_type=jnp.float32).astype(jnp.bfloat16)


def expert_backward(row_block, stash_rows, gate_part, up_part, down_part):
    hid_count = gate_part.shape[1]
    contract = (((1,), (1,)), ((), ()))
    gate_pre = stash_rows[:, :hid_count].astype(jnp.float32)
    up_pre = stash_rows[:, hid_count:].astype(jnp.float32)
    grad_hidden = lax.dot_general(
        row_block, down_part, contract, preferred_element_type=jnp.float32
    )
    sigmoid_a = jax.nn.sigmoid(gate_pre)
    grad_gate = (grad_hidden * up_pre * sigmoid_a * (1.0 + gate_pre * (1.0 - sigmoid_a))).astype(
        jnp.bfloat16
    )
    grad_up = (grad_hidden * gate_pre * sigmoid_a).astype(jnp.bfloat16)
    part_grad = lax.dot_general(grad_gate, gate_part, contract, preferred_element_type=jnp.float32)
    part_grad = part_grad + lax.dot_general(
        grad_up, up_part, contract, preferred_element_type=jnp.float32
    )
    return part_grad.astype(jnp.bfloat16)


def on_device(
    fwd_in,
    gains,
    gate_weight,
    up_weight,
    down_weight,
    fwd_routes,
    fwd_probs,
    bwd_grad,
    bwd_input,
    bwd_routes,
    bwd_probs,
    bwd_stash,
):
    groups = lax.axis_size("expert")
    experts = groups // SPLIT
    capacity = bwd_stash.shape[1] // groups
    norm_gain = gains[0]
    gate_part = gate_weight[0]
    up_part = up_weight[0]
    down_part = down_weight[0]
    arrived = passed_along(fwd_in[0], "section", 1)
    upstream = passed_along(bwd_grad[0], "section", -1)
    normed = rms_scale(arrived.astype(jnp.float32), norm_gain).astype(jnp.bfloat16)
    fwd_buffer, fwd_index = slot_layout(fwd_routes[0], experts, capacity, normed)
    bwd_buffer, bwd_index = slot_layout(bwd_routes[0], experts, capacity, upstream)
    stash_rows = bwd_stash[0]
    fwd_rows = dispatch(fwd_buffer, experts, capacity)
    fwd_totals = send_back(
        expert_forward(fwd_rows, gate_part, up_part, down_part), experts, capacity
    )
    bwd_rows = dispatch(bwd_buffer, experts, capacity)
    bwd_totals = send_back(
        expert_backward(bwd_rows, stash_rows, gate_part, up_part, down_part), experts, capacity
    )
    mixture = combine_rows(fwd_totals, fwd_index, fwd_probs[0])
    fwd_result = (arrived.astype(jnp.float32) + mixture).astype(jnp.bfloat16)
    grad_normed = combine_rows(bwd_totals, bwd_index, bwd_probs[0])
    _, pullback = jax.vjp(
        lambda value: rms_scale(value, norm_gain), bwd_input[0].astype(jnp.float32)
    )
    grad_input = pullback(grad_normed)[0]
    bwd_result = (upstream.astype(jnp.float32) + grad_input).astype(jnp.bfloat16)
    return (fwd_result[None], bwd_result[None])


def solution(mesh):
    return jax.shard_map(
        on_device,
        mesh=mesh,
        in_specs=(
            P("section", "expert", None),
            P("section", None),
            P("section", None, "expert"),
            P("section", None, "expert"),
            P("section", "expert", None),
            P("section", "expert", None),
            P("section", "expert", None),
            P("section", "expert", None),
            P("section", "expert", None),
            P("section", "expert", None),
            P("section", "expert", None),
            P("section", "expert", None),
        ),
        out_specs=(P("section", "expert", None), P("section", "expert", None)),
        check_vma=False,
    )
```

profile of v0, /device:TPU:29, one launch (start us, length us, event | category | flops | bytes accessed | tf_op | source)
XLA Modules:
  0.0 846.4 jit_solution(1198130007931773457)
XLA Ops:
  3.7 10.0 %collective-permute-done.1 = bf16[64,7168]{1,0:T(8,128)(2,1)S(1)} collective-permute-done((bf16[64,7168]{1,0:T(8,128)(2,1)}, bf16[64,7168]{1,0:T(8,128)(2,1)S(1)}, u32[]{:S(2)}, u32[]{:S(2)}) %collective-permute-start.1) | collective-permute-done | bytes 917536 | tf_op jit(solution)/shard_map/ppermute | solution.py:15
  13.7 0.9 copy-done.5
  14.7 2.2 convolution_convert_fusion.1
  16.9 2.6 broadcast_in_dim.17
  19.5 5.4 broadcast_in_dim.18
  24.9 10.3 %all-to-all-start.2 = ((bf16[32,20,7168]{2,1,0:T(8,128)(2,1)}), bf16[32,20,7168]{2,1,0:T(8,128)(2,1)}, u32[]{:S(2)}, u32[]{:S(2)}) async-start(bf16[32,20,7168]{2,1,0:T(8,128)(2,1)} %bitcast.76), calls=%async_computation.2 | async-start | bytes 22020096 | tf_op jit(solution)/shard_map/all_to_all | solution.py:50
  36.8 156.5 %collective-permute-done = bf16[64,7168]{1,0:T(8,128)(2,1)S(1)} collective-permute-done((bf16[64,7168]{1,0:T(8,128)(2,1)S(1)}, bf16[64,7168]{1,0:T(8,128)(2,1)S(1)}, u32[]{:S(2)}, u32[]{:S(2)}) %collective-permute-start) | collective-permute-done | bytes 917536 | tf_op jit(solution)/shard_map/ppermute | solution.py:15
  194.2 2.2 convolution_convert_fusion.2
  196.5 2.6 broadcast_in_dim.14
  199.1 20.1 %all-to-all-done.2 = bf16[32,20,7168]{2,1,0:T(8,128)(2,1)} async-done(((bf16[32,20,7168]{2,1,0:T(8,128)(2,1)}), bf16[32,20,7168]{2,1,0:T(8,128)(2,1)}, u32[]{:S(2)}, u32[]{:S(2)}) %all-to-all-start.2) | async-done | bytes 9175072 | tf_op jit(solution)/shard_map/all_to_all | solution.py:50
  219.2 5.4 broadcast_in_dim.15
  224.6 21.2 %all-to-all-start = ((bf16[32,20,7168]{2,1,0:T(8,128)(2,1)}), bf16[32,20,7168]{2,1,0:T(8,128)(2,1)}, u32[]{:S(2)}, u32[]{:S(2)}) async-start(bf16[32,20,7168]{2,1,0:T(8,128)(2,1)} %bitcast.77), calls=%async_computation | async-start | bytes 22020096 | tf_op jit(solution)/shard_map/all_to_all | solution.py:50
  245.9 13.3 %all_to_all.28 = bf16[640,7168]{1,0:T(8,128)(2,1)} reshape(bf16[32,20,7168]{2,1,0:T(8,128)(2,1)} %all-to-all-done.2) | data formatting | bytes 18350080 | tf_op jit(solution)/shard_map/all_to_all | solution.py:50
  259.2 7.4 fusion.2
  266.6 9.0 %fusion.8 = f32[640,7168]{1,0:T(8,128)} fusion(bf16[1,7168,256]{2,1,0:T(8,128)(2,1)S(1)} %copy-done.3, f32[640,256]{1,0:T(8,128)S(1)} %fusion.2, bf16[640,512]{1,0:T(8,128)(2,1)S(1)} %bitcast.78), kind=kOutput, calls=%fused_computation.16 | convolution fusion | flops 2350776320 | bytes 23330816 | tf_op jit(solution)/shard_map/dot_general | solution.py:95
  275.6 11.3 %fusion.1 = bf16[1,640,7168]{2,1,0:T(8,128)(2,1)} fusion(f32[640,7168]{1,0:T(8,128)} %fusion.8, bf16[1,7168,256]{2,1,0:T(8,128)(2,1)} %param.15, f32[640,256]{1,0:T(8,128)S(1)} %fusion.2, bf16[640,512]{1,0:T(8,128)(2,1)S(1)} %bitcast.79), kind=kOutput, calls=%fused_computation.7 | convolution fusion | flops 2359132160 | bytes 32178176 | tf_op jit(solution)/shard_map/dot_general | solution.py:96
  286.8 16.9 %copy.60 = bf16[1,640,7168]{2,0,1:T(2,128)(2,1)} copy(bf16[1,640,7168]{2,1,0:T(8,128)(2,1)} %fusion.1) | data formatting | bytes 18350080 | tf_op jit(solution)/shard_map/reshape | solution.py:61
  304.3 54.0 %reduce.5 = bf16[640,7168]{1,0:T(8,128)(2,1)} reduce(bf16[640,1,7168]{2,1,0:T(2,128)(2,1)} %bitcast.74, bf16[]{:T(256)} %broadcast.166), dimensions={1}, to_apply=%bitcast.72.reduce_sub_computation | reduce | bytes 18350082
  358.3 14.7 %reshape.195 = bf16[32,2,71680]{2,1,0:T(2,128)(2,1)} reshape(bf16[640,7168]{1,0:T(8,128)(2,1)} %reduce.5) | data formatting | bytes 18350080
  373.0 27.8 %all-to-all-done = bf16[32,20,7168]{2,1,0:T(8,128)(2,1)} async-done(((bf16[32,20,7168]{2,1,0:T(8,128)(2,1)}), bf16[32,20,7168]{2,1,0:T(8,128)(2,1)}, u32[]{:S(2)}, u32[]{:S(2)}) %all-to-all-start) | async-done | bytes 9175072 | tf_op jit(solution)/shard_map/all_to_all | solution.py:50
  400.8 8.6 %all-to-all-start.3 = ((bf16[32,2,71680]{2,1,0:T(2,128)(2,1)}), bf16[32,2,71680]{2,1,0:T(2,128)(2,1)}, u32[]{:S(2)}, u32[]{:S(2)}) async-start(bf16[32,2,71680]{2,1,0:T(2,128)(2,1)} %reshape.195), calls=%async_computation.3 | async-start | bytes 18350080 | tf_op jit(solution)/shard_map/all_to_all | solution.py:62
  409.4 13.3 %all_to_all.24 = bf16[640,7168]{1,0:T(8,128)(2,1)} reshape(bf16[32,20,7168]{2,1,0:T(8,128)(2,1)} %all-to-all-done) | data formatting | bytes 18350080 | tf_op jit(solution)/shard_map/all_to_all | solution.py:50
  422.7 7.2 fusion.10
  429.9 19.0 %fusion = bf16[1,640,7168]{2,1,0:T(8,128)(2,1)} fusion(bf16[1,256,7168]{2,1,0:T(8,128)(2,1)} %param.16, bf16[640,7168]{1,0:T(8,128)(2,1)} %all_to_all.24, bf16[1,7168,256]{2,1,0:T(8,128)(2,1)} %param.15, f32[640,256]{1,0:T(8,128)S(1)} %fusion.10), kind=kOutput, calls=%fused_computation.6 | convolution fusion | flops 4703191040 | bytes 26345472 | tf_op jit(solution)/shard_map/dot_general | solution.py:79
  448.9 16.9 %copy.61 = bf16[1,640,7168]{2,0,1:T(2,128)(2,1)} copy(bf16[1,640,7168]{2,1,0:T(8,128)(2,1)} %fusion) | data formatting | bytes 18350080 | tf_op jit(solution)/shard_map/reshape | solution.py:61
  465.8 54.1 %reduce.4 = bf16[640,7168]{1,0:T(8,128)(2,1)} reduce(bf16[640,1,7168]{2,1,0:T(2,128)(2,1)} %bitcast.75, bf16[]{:T(256)} %broadcast.166), dimensions={1}, to_apply=%bitcast.73.reduce_sub_computation | reduce | bytes 18350082
  519.9 14.6 %reshape.193 = bf16[32,2,71680]{2,1,0:T(2,128)(2,1)} reshape(bf16[640,7168]{1,0:T(8,128)(2,1)} %reduce.4) | data formatting | bytes 18350080
  534.5 8.5 %all-to-all-done.3 = bf16[32,2,71680]{2,1,0:T(2,128)(2,1)} async-done(((bf16[32,2,71680]{2,1,0:T(2,128)(2,1)}), bf16[32,2,71680]{2,1,0:T(2,128)(2,1)}, u32[]{:S(2)}, u32[]{:S(2)}) %all-to-all-start.3) | async-done | bytes 9175072 | tf_op jit(solution)/shard_map/all_to_all | solution.py:62
  543.0 9.1 %all-to-all-start.1 = ((bf16[32,2,71680]{2,1,0:T(2,128)(2,1)}), bf16[32,2,71680]{2,1,0:T(2,128)(2,1)}, u32[]{:S(2)}, u32[]{:S(2)}) async-start(bf16[32,2,71680]{2,1,0:T(2,128)(2,1)} %reshape.193), calls=%async_computation.1 | async-start | bytes 18350080 | tf_op jit(solution)/shard_map/all_to_all | solution.py:62
  552.9 24.1 %reshape.196 = bf16[640,1,7168]{2,1,0:T(2,128)(2,1)} reshape(bf16[32,2,71680]{2,1,0:T(2,128)(2,1)} %all-to-all-done.3) | data formatting | bytes 18350080
  577.0 60.8 %convert_reduce_fusion = f32[640,7168]{1,0:T(8,128)} fusion(bf16[640,1,7168]{2,1,0:T(2,128)(2,1)} %reshape.196), kind=kLoop, calls=%fused_computation.2 | loop fusion | flops 4587520 | bytes 27525120 | tf_op jit(solution)/shard_map/convert_element_type | solution.py:64
  637.8 19.0 %reshape.173 = f32[8,4,20,7168]{3,2,1,0:T(8,128)} reshape(f32[640,7168]{1,0:T(8,128)} %convert_reduce_fusion) | data formatting | bytes 36700160 | tf_op jit(solution)/shard_map/convert_element_type | solution.py:64
  656.7 11.4 %reduce_sum.101 = f32[8,20,7168]{2,1,0:T(8,128)} reduce(f32[8,4,20,7168]{3,2,1,0:T(8,128)} %reshape.173, f32[]{:T(128)} %constant.24.clone.1), dimensions={1}, to_apply=%region_9.10 | reduce | flops 3440640 | bytes 22937604 | tf_op jit(solution)/shard_map/reduce_sum | solution.py:63
  668.2 5.2 reshape.170
  673.4 7.3 gather_fusion.1
  680.7 5.5 reshape.171
  686.2 10.7 %all-to-all-done.1 = bf16[32,2,71680]{2,1,0:T(2,128)(2,1)} async-done(((bf16[32,2,71680]{2,1,0:T(2,128)(2,1)}), bf16[32,2,71680]{2,1,0:T(2,128)(2,1)}, u32[]{:S(2)}, u32[]{:S(2)}) %all-to-all-start.1) | async-done | bytes 9175072 | tf_op jit(solution)/shard_map/all_to_all | solution.py:62
  696.9 24.1 %reshape.194 = bf16[640,1,7168]{2,1,0:T(2,128)(2,1)} reshape(bf16[32,2,71680]{2,1,0:T(2,128)(2,1)} %all-to-all-done.1) | data formatting | bytes 18350080
  721.0 60.8 %convert_reduce_fusion.1 = f32[640,7168]{1,0:T(8,128)} fusion(bf16[640,1,7168]{2,1,0:T(2,128)(2,1)} %reshape.194), kind=kLoop, calls=%fused_computation.3 | loop fusion | flops 4587520 | bytes 27525120 | tf_op jit(solution)/shard_map/convert_element_type | solution.py:64
  781.7 19.0 %reshape.172 = f32[8,4,20,7168]{3,2,1,0:T(8,128)} reshape(f32[640,7168]{1,0:T(8,128)} %convert_reduce_fusion.1) | data formatting | bytes 36700160 | tf_op jit(solution)/shard_map/convert_element_type | solution.py:64
  800.7 11.7 %reduce_sum.96 = f32[8,20,7168]{2,1,0:T(8,128)} reduce(f32[8,4,20,7168]{3,2,1,0:T(8,128)} %reshape.172, f32[]{:T(128)} %constant.24.clone.1), dimensions={1}, to_apply=%region_4.5 | reduce | flops 3440640 | bytes 22937604 | tf_op jit(solution)/shard_map/reduce_sum | solution.py:63
  812.4 5.2 reshape.167
  817.6 7.3 gather_fusion
  824.9 5.5 reshape.168
  830.4 7.3 multiply_reduce_fusion
  838.4 5.1 multiply_reduce_fusion.1
  843.6 1.1 fusion.29
  844.6 1.5 fusion.28
  (66 shorter events, 7.5 us)
Async XLA Ops:
  0.6 13.1 %collective-permute-start.1 = (bf16[64,7168]{1,0:T(8,128)(2,1)}, bf16[64,7168]{1,0:T(8,128)(2,1)S(1)}, u32[]{:S(2)}, u32[]{:S(2)}) collective-permute-start(bf16[64,7168]{1,0:T(8,128)(2,1)} %bitcast.85), channel_id=1, source_target_pairs={{32,0},{64,32},{96,64},{0,96},{33,1},{65,33},{97,65},{1,97},{34,2}... | collective-permute-start | bytes 2752520 | tf_op jit(solution)/shard_map/ppermute | solution.py:15
  13.7 0.9 copy-start.5
  24.9 10.4 %copy-start.14 = (bf16[1,64,7168]{2,1,0:T(8,128)(2,1)S(1)}, bf16[1,64,7168]{2,1,0:T(8,128)(2,1)}, u32[]{:S(2)}) copy-start(bf16[1,64,7168]{2,1,0:T(8,128)(2,1)} %param.12) | copy-start | bytes 2752516
  24.9 10.9 %copy-start.11 = (s32[1,64,2]{1,2,0:T(2,128)S(1)}, s32[1,64,2]{1,2,0:T(2,128)}, u32[]{:S(2)}) copy-start(s32[1,64,2]{1,2,0:T(2,128)} %param.17) | copy-start | bytes 1540
  24.9 169.4 %copy-start.8 = (f32[1,7168]{1,0:T(1,128)S(1)}, f32[1,7168]{1,0:T(1,128)}, u32[]{:S(2)}) copy-start(f32[1,7168]{1,0:T(1,128)} %param.13) | copy-start | bytes 86020
  24.9 194.3 %all-to-all-start.2 = ((bf16[32,20,7168]{2,1,0:T(8,128)(2,1)}), bf16[32,20,7168]{2,1,0:T(8,128)(2,1)}, u32[]{:S(2)}, u32[]{:S(2)}) async-start(bf16[32,20,7168]{2,1,0:T(8,128)(2,1)} %bitcast.76), calls=%async_computation.2 | async-start | bytes 22020096 | tf_op jit(solution)/shard_map/all_to_all | solution.py:50
  35.2 158.1 %collective-permute-start = (bf16[64,7168]{1,0:T(8,128)(2,1)S(1)}, bf16[64,7168]{1,0:T(8,128)(2,1)S(1)}, u32[]{:S(2)}, u32[]{:S(2)}) collective-permute-start(bf16[64,7168]{1,0:T(8,128)(2,1)S(1)} %bitcast.86), channel_id=1, source_target_pairs={{96,0},{0,32},{32,64},{64,96},{97,1},{1,33},{33,65},{65,97},{98,2}... | collective-permute-start | bytes 2752520 | tf_op jit(solution)/shard_map/ppermute | solution.py:15
  193.3 0.9 copy-start.1
  224.6 176.2 %all-to-all-start = ((bf16[32,20,7168]{2,1,0:T(8,128)(2,1)}), bf16[32,20,7168]{2,1,0:T(8,128)(2,1)}, u32[]{:S(2)}, u32[]{:S(2)}) async-start(bf16[32,20,7168]{2,1,0:T(8,128)(2,1)} %bitcast.77), calls=%async_computation | async-start | bytes 22020096 | tf_op jit(solution)/shard_map/all_to_all | solution.py:50
  259.2 7.4 copy-start.3
  259.2 7.4 copy-start.7
  400.8 142.2 %all-to-all-start.3 = ((bf16[32,2,71680]{2,1,0:T(2,128)(2,1)}), bf16[32,2,71680]{2,1,0:T(2,128)(2,1)}, u32[]{:S(2)}, u32[]{:S(2)}) async-start(bf16[32,2,71680]{2,1,0:T(2,128)(2,1)} %reshape.195), calls=%async_computation.3 | async-start | bytes 18350080 | tf_op jit(solution)/shard_map/all_to_all | solution.py:62
  534.5 17.6 %copy-start.10 = (s32[1,64,2]{1,2,0:T(2,128)S(1)}, s32[1,64,2]{1,2,0:T(2,128)}, u32[]{:S(2)}) copy-start(s32[1,64,2]{1,2,0:T(2,128)} %param.21) | copy-start | bytes 1540
  534.5 17.8 %copy-start.12 = (f32[1,64,2]{1,2,0:T(2,128)S(1)}, f32[1,64,2]{1,2,0:T(2,128)}, u32[]{:S(2)}) copy-start(f32[1,64,2]{1,2,0:T(2,128)} %param.22) | copy-start | bytes 1540
  534.5 18.2 %copy-start.13 = (f32[1,64,2]{1,2,0:T(2,128)S(1)}, f32[1,64,2]{1,2,0:T(2,128)}, u32[]{:S(2)}) copy-start(f32[1,64,2]{1,2,0:T(2,128)} %param.18) | copy-start | bytes 1540
  543.0 153.9 %all-to-all-start.1 = ((bf16[32,2,71680]{2,1,0:T(2,128)(2,1)}), bf16[32,2,71680]{2,1,0:T(2,128)(2,1)}, u32[]{:S(2)}, u32[]{:S(2)}) async-start(bf16[32,2,71680]{2,1,0:T(2,128)(2,1)} %reshape.193), calls=%async_computation.1 | async-start | bytes 18350080 | tf_op jit(solution)/shard_map/all_to_all | solution.py:62
  830.4 7.3 copy-start.4
  830.4 7.3 copy-start.9
  830.4 8.0 copy-start
  837.7 5.8 copy-start.2
  838.4 6.3 copy-start.6
where the time goes:
time: 856 us; the launch traced here: 846 us
  other arithmetic  270 us (32%)
  waiting for transfers between devices  234 us (27%)
  local copies, waits for them, and re-layouts  232 us (27%)
  matrix products  58.2 us (7%)
  starting transfers between devices  50.6 us (6%)
    ppermute x2, waiting for transfers between devices, passed_along(): return lax.ppermute(block, axis, route)  166 us
    convert_element_type x2, other arithmetic, send_back(): returned.reshape(experts, SPLIT, capacity, feature).astype(jnp.float32)  122 us
    unnamed x2, other arithmetic  108 us
    unnamed x37, local copies, waits for them, and re-layouts  80.6 us
    all_to_all x2, waiting for transfers between devices, dispatch(): lax.all_to_all(copies.reshape(experts * SPLIT * capacity, feature), 'expe...  47.9 us
    convert_element_type x2, local copies, waits for them, and re-layouts, send_back(): returned.reshape(experts, SPLIT, capacity, feature).astype(jnp.float32)  38 us
    reshape x2, local copies, waits for them, and re-layouts, send_back(): shaped = partial_rows.reshape(1, experts * SPLIT * capacity, feature)  33.9 us
    all_to_all x2, starting transfers between devices, dispatch(): lax.all_to_all(copies.reshape(experts * SPLIT * capacity, feature), 'expe...  31.6 us
  transfers between devices with their start and end apart: 6, of which 6 were waited for; matrix products, arithmetic and copies ran while one was open for 43% of the time, Pallas kernels for 0%

commit v1 on v0

v1 whole, which is shorter than its diff:
```python
import functools

import jax
import jax.numpy as jnp
import numpy as np
from jax import lax
from jax.experimental import pallas as pl
from jax.experimental.pallas import tpu as pltpu
from jax.sharding import PartitionSpec as P

EPSILON = 1e-06
MESH = pl.DeviceIdType.MESH
CAP = 20
CHUNK = 1024
PIECE = 512
NT = (((1,), (1,)), ((), ()))


def mm(a, b):
    return jnp.dot(a, b, preferred_element_type=jnp.float32)


def mm_t(a, b):
    return lax.dot_general(a, b, NT, preferred_element_type=jnp.float32)


def slot_keys(routes, offset):
    tokens = routes.shape[0]
    lane = lax.broadcasted_iota(jnp.int32, (tokens, 128), 1)
    first, second = routes[:, 0:1], routes[:, 1:2]
    one0 = jnp.where(first == lane, 1.0, 0.0)
    one1 = jnp.where(second == lane, 1.0, 0.0)
    row = lax.broadcasted_iota(jnp.int32, (tokens, tokens), 0)
    col = lax.broadcasted_iota(jnp.int32, (tokens, tokens), 1)
    lower = jnp.where(col < row, 1.0, 0.0).astype(jnp.bfloat16)
    before = mm(lower, (one0 + one1).astype(jnp.bfloat16))
    pos0 = jnp.sum(one0 * before, axis=1, keepdims=True)
    pos1 = jnp.sum(one1 * before, axis=1, keepdims=True)
    key0 = first.astype(jnp.float32) * CAP + pos0 + offset
    key1 = second.astype(jnp.float32) * CAP + pos1 + offset
    return key0, key1


def kernel(
    fwd_in, bwd_grad, gains, wg, wu, wd, f_routes, f_probs, b_routes, b_probs, bwd_input, stash, target,
    fwd_out, bwd_out,
    meta, dense, packed, rows, back, o_recv, x_recv, wd_own, wd_peer, w_own, w_peer,
    st_own, st_peer, acc, small, hid, pack, comb, pend, pend2, grad,
    relay_s, relay_r, meta_s, meta_r, o_s, o_r, z_s, z_r, wt_s, wt_r, wd_s, wd_r, st_s, st_r,
    zb_s, zb_r, ob_s, ob_r, xb_s, xb_r, loc, zloc, wloc, zbloc,
):
    depth = fwd_in.shape[1]
    chunks = depth // CHUNK
    hidden = wg.shape[1]
    sec = lax.axis_index("section")
    ex = lax.axis_index("expert")
    z, y, x = ex // 8, (ex // 2) % 4, ex % 2
    half = y // 2
    cls = ((y + 1) // 2) % 2
    own = pl.multiple_of(half * 128, 128)
    other = pl.multiple_of((1 - half) * 128, 128)
    mine = pl.multiple_of(half * 128 + x * 64, 64)
    up, down = (sec + 1) % 4, (sec + 3) % 4

    def at(zz, yy, xx):
        return zz * 8 + yy * 2 + xx

    x_peer = (sec, at(z, y, 1 - x))
    o_peer = (sec, at(z, 3 - y, x))
    d_peer = (sec, at(z, 3 - y, 1 - x))
    i_peer = (sec, at(z, y + 1 - 2 * (y % 2), x))
    z_peers = [(sec, at((z + d) % 4, y, x)) for d in (1, 2, 3)]
    relays = [(s, at(z, y, xx)) for s in (up, down) for xx in (x, 1 - x)]

    barrier = pltpu.get_barrier_semaphore()
    partners = [x_peer, o_peer, d_peer, i_peer] + z_peers + relays
    for peer in partners:
        pl.semaphore_signal(barrier, inc=1, device_id=peer, device_id_type=MESH)
    pl.semaphore_wait(barrier, len(partners))

    def remote(src, dst, send, recv, peer):
        return pltpu.make_async_remote_copy(
            src_ref=src, dst_ref=dst, send_sem=send, recv_sem=recv, device_id=peer, device_id_type=MESH
        )

    def relay(flow):
        src = (bwd_grad, fwd_in)[flow]
        sec_to = (down, up)[flow]
        return [
            remote(src, dense.at[flow, pl.ds(mine, 64)], relay_s.at[flow, d], relay_r.at[flow, d], (sec_to, at(z, y, xx)))
            for d, xx in enumerate((x, 1 - x))
        ]

    bwd_relay, fwd_relay = relay(0), relay(1)
    for copy in bwd_relay:
        copy.start()
    st_copy = remote(
        stash.at[pl.ds(pl.multiple_of((1 - cls) * 320, 320), 320)], st_peer, st_s, st_r, i_peer
    )
    st_copy.start()
    wd_copy = remote(wd, wd_peer, wd_s, wd_r, i_peer)
    wd_copy.start()

    def w_copies(c):
        at_c = pl.ds(pl.multiple_of(c * CHUNK, CHUNK), CHUNK)
        return [
            remote(w.at[at_c], w_peer.at[k, at_c], wt_s.at[k, c], wt_r.at[k, c], i_peer)
            for k, w in enumerate((wg, wu))
        ]

    def w_send(c):
        for copy in w_copies(c):
            copy.start()

    def w_load(c):
        at_c = pl.ds(pl.multiple_of(c * CHUNK, CHUNK), CHUNK)
        return [
            pltpu.make_async_copy(w.at[at_c], w_own.at[c % 2, k], wloc.at[c % 2, k])
            for k, w in enumerate((wg, wu))
        ]

    st_load = pltpu.make_async_copy(stash.at[pl.ds(pl.multiple_of(cls * 320, 320), 320)], st_own, loc.at[0])
    st_load.start()
    wd_load = pltpu.make_async_copy(wd, wd_own, loc.at[1])
    wd_load.start()
    for copy in w_load(0):
        copy.start()

    lane = lax.broadcasted_iota(jnp.int32, (64, 128), 1)
    offset = ((half * 2 + x) * 1000).astype(jnp.float32)
    columns = []
    for routes, probs in ((b_routes, b_probs), (f_routes, f_probs)):
        key0, key1 = slot_keys(routes[...], offset)
        columns += [key0, key1, probs[:, 0:1], probs[:, 1:2]]
    value = jnp.zeros((64, 128), jnp.float32)
    for i, column in enumerate(columns):
        value = jnp.where(lane == i, column, value)
    meta[pl.ds(mine, 64)] = value
    meta_copies = [
        remote(meta.at[pl.ds(mine, 64)], meta.at[pl.ds(mine, 64)], meta_s.at[i], meta_r.at[i], peer)
        for i, peer in enumerate((x_peer, o_peer, d_peer))
    ]
    for copy in meta_copies:
        copy.start()

    def o_copy(flow):
        block = dense.at[flow, pl.ds(own, 128)]
        return remote(block, block, o_s.at[flow], o_r.at[flow], o_peer)

    for copy in bwd_relay:
        copy.wait()
    o_copy(0).start()
    for copy in fwd_relay:
        copy.start()
    w_send(0)
    bwd_out[...] = dense[0, pl.ds(mine, 64)]

    for copy in meta_copies:
        copy.wait()
    goal = target[...] + (half * CAP).astype(jnp.float32)
    for flow in range(2):
        base = flow * 4
        one0 = jnp.where(meta[:, base : base + 1] == goal, 1.0, 0.0)
        one1 = jnp.where(meta[:, base + 1 : base + 2] == goal, 1.0, 0.0)
        pack[flow] = jnp.transpose(one0 + one1).astype(jnp.bfloat16)
        weight = one0 * meta[:, base + 2 : base + 3] + one1 * meta[:, base + 3 : base + 4]
        high = weight.astype(jnp.bfloat16)
        comb[flow, 0] = high
        comb[flow, 1] = (weight - high.astype(jnp.float32)).astype(jnp.bfloat16)

    for copy in fwd_relay:
        copy.wait()
    fwd_out[...] = dense[1, pl.ds(mine, 64)]

    def norm_rows(i, carry):
        at_i = pl.ds(pl.multiple_of(half * 128 + i * 16, 16), 16)
        v = dense[1, at_i].astype(jnp.float32)
        scale = lax.rsqrt(jnp.mean(v * v, axis=1, keepdims=True) + EPSILON)
        dense[1, at_i] = (v * scale * gains[...]).astype(jnp.bfloat16)
        return carry

    lax.fori_loop(0, 8, norm_rows, 0)
    o_copy(1).start()
    w_send(1)

    def z_copies(flow):
        return [
            remote(
                packed.at[pl.ds(pl.multiple_of(((z + d) % 4) * 80, 80), 80)],
                rows.at[flow, pl.ds(pl.multiple_of(z * 80, 80), 80)],
                z_s.at[flow, d - 1], z_r.at[flow, d - 1], z_peers[d - 1],
            )
            for d in (1, 2, 3)
        ]

    def z_local(flow):
        at_z = pl.ds(pl.multiple_of(z * 80, 80), 80)
        return pltpu.make_async_copy(packed.at[at_z], rows.at[flow, at_z], zloc.at[flow])

    def pack_rows(flow):
        def step(c, carry):
            at_c = pl.ds(pl.multiple_of(c * PIECE, PIECE), PIECE)
            packed[:, at_c] = mm(pack[flow, 0:320], dense[flow, :, at_c]).astype(jnp.bfloat16)
            return carry

        lax.fori_loop(0, depth // PIECE, step, 0)
        for copy in z_copies(flow):
            copy.start()
        z_local(flow).start()

    o_copy(0).wait()
    pack_rows(0)
    w_send(2)
    o_copy(1).wait()
    for copy in z_copies(0):
        copy.wait_send()
    z_local(0).wait()
    pack_rows(1)
    w_send(3)

    for copy in z_copies(0):
        copy.wait_recv()
    wd_load.wait()
    wd_copy.wait()
    acc[...] = jnp.zeros_like(acc)

    def hid_grad(c, carry):
        at_c = pl.ds(pl.multiple_of(c * CHUNK, CHUNK), CHUNK)
        block = rows[0, :, at_c]
        acc[0, 0] += mm_t(block, wd_own[:, at_c])
        acc[0, 1] += mm_t(block, wd_peer[:, at_c])
        return carry

    lax.fori_loop(0, chunks, hid_grad, 0)
    st_load.wait()
    st_copy.wait()
    for k, st in enumerate((st_own, st_peer)):
        a = st[:, 0:hidden].astype(jnp.float32)
        b = st[:, hidden : 2 * hidden].astype(jnp.float32)
        sig = jax.nn.sigmoid(a)
        g = acc[0, k]
        small[0, k] = (g * b * sig * (1.0 + a * (1.0 - sig))).astype(jnp.bfloat16)
        small[1, k] = (g * a * sig).astype(jnp.bfloat16)
    acc[...] = jnp.zeros_like(acc)

    u_load = pltpu.make_async_copy(bwd_input, packed.at[0:64], loc.at[2])

    def zb_copies(q):
        flow, c = q // chunks, q % chunks
        at_c = pl.ds(pl.multiple_of(c * CHUNK, CHUNK), CHUNK)
        return [
            remote(
                rows.at[flow, pl.ds(pl.multiple_of(((z + d) % 4) * 80, 80), 80), at_c],
                back.at[flow, pl.ds(pl.multiple_of(z * 80, 80), 80), at_c],
                zb_s.at[q, d - 1], zb_r.at[q, d - 1], z_peers[d - 1],
            )
            for d in (1, 2, 3)
        ]

    def zb_local(q):
        flow, c = q // chunks, q % chunks
        at_c = pl.ds(pl.multiple_of(c * CHUNK, CHUNK), CHUNK)
        at_z = pl.ds(pl.multiple_of(z * 80, 80), 80)
        return pltpu.make_async_copy(rows.at[flow, at_z, at_c], back.at[flow, at_z, at_c], zbloc.at[q])

    def ob_copy(q):
        flow, c = q // chunks, q % chunks
        at_c = pl.ds(pl.multiple_of(c * CHUNK, CHUNK), CHUNK)
        return remote(dense.at[flow, pl.ds(0, 128), at_c], o_recv.at[flow, :, at_c], ob_s.at[q], ob_r.at[q], o_peer)

    def xb_copy(q):
        flow, c = q // chunks, q % chunks
        at_c = pl.ds(pl.multiple_of(c * CHUNK, CHUNK), CHUNK)
        return remote(dense.at[flow, pl.ds(128, 64), at_c], x_recv.at[flow, :, at_c], xb_s.at[q], xb_r.at[q], x_peer)

    def send_back(q):
        for copy in zb_copies(q):
            copy.start()
        zb_local(q).start()

    def step(t, carry):
        at_t = pl.ds(pl.multiple_of((t % chunks) * CHUNK, CHUNK), CHUNK)

        @pl.when(t < chunks)
        def _():
            for copy in w_copies(t):
                copy.wait()
            for copy in w_load(t):
                copy.wait()

            @pl.when(t + 4 < chunks)
            def _():
                w_send(t + 4)

            @pl.when(t + 1 < chunks)
            def _():
                for copy in w_load(t + 1):
                    copy.start()

            def out_grad(i, carry):
                at_i = pl.ds(pl.multiple_of(i * PIECE, PIECE), PIECE)
                at_p = pl.ds(pl.multiple_of(t * CHUNK + i * PIECE, PIECE), PIECE)
                total = mm_t(small[0, 0], w_own[t % 2, 0, at_i]) + mm_t(small[1, 0], w_own[t % 2, 1, at_i])
                total += mm_t(small[0, 1], w_peer[0, at_p])
                total += mm_t(small[1, 1], w_peer[1, at_p])
                rows[0, :, at_p] = total.astype(jnp.bfloat16)
                return carry

            lax.fori_loop(0, CHUNK // PIECE, out_grad, 0)
            send_back(t)

            @pl.when(t == 0)
            def _():
                for copy in z_copies(1):
                    copy.wait()
                z_local(1).wait()
                u_load.start()

            block = rows[1, :, at_t]
            for k in range(2):
                acc[k, 0] += mm(block, w_own[t % 2, k])
                acc[k, 1] += mm(block, w_peer[k, at_t])

        @pl.when(t == chunks)
        def _():
            for k in range(2):
                gate = acc[0, k]
                hid[k] = (gate * jax.nn.sigmoid(gate) * acc[1, k]).astype(jnp.bfloat16)

        @pl.when((t >= chunks) & (t < 2 * chunks))
        def _():
            def out_rows(i, carry):
                at_p = pl.ds(pl.multiple_of((t - chunks) * CHUNK + i * PIECE, PIECE), PIECE)
                total = mm(hid[0], wd_own[:, at_p]) + mm(hid[1], wd_peer[:, at_p])
                rows[1, :, at_p] = total.astype(jnp.bfloat16)
                return carry

            lax.fori_loop(0, CHUNK // PIECE, out_rows, 0)
            send_back(t)

        @pl.when((t >= 2) & (t < 2 * chunks + 2))
        def _():
            q = t - 2
            flow = q // chunks
            at_c = pl.ds(pl.multiple_of((q % chunks) * CHUNK, CHUNK), CHUNK)
            for copy in zb_copies(q):
                copy.wait()
            zb_local(q).wait()
            block = back[flow, :, at_c]
            away = mm(comb[flow, 0, pl.ds(other, 128), 0:320], block)
            away += mm(comb[flow, 1, pl.ds(other, 128), 0:320], block)
            dense[flow, 0:128, at_c] = away.astype(jnp.bfloat16)
            ob_copy(q).start()
            keep = mm(comb[flow, 0, pl.ds(own, 128), 0:320], block)
            keep += mm(comb[flow, 1, pl.ds(own, 128), 0:320], block)
            pend[q % 3] = keep

        @pl.when((t >= 4) & (t < 2 * chunks + 4))
        def _():
            q = t - 4
            flow = q // chunks
            at_c = pl.ds(pl.multiple_of((q % chunks) * CHUNK, CHUNK), CHUNK)
            ob_copy(q).wait()
            pend[q % 3] += o_recv[flow, :, at_c].astype(jnp.float32)
            dense[flow, 128:192, at_c] = pend[q % 3, pl.ds(pl.multiple_of((1 - x) * 64, 64), 64)].astype(jnp.bfloat16)
            xb_copy(q).start()
            pend2[q % 3] = pend[q % 3, pl.ds(pl.multiple_of(x * 64, 64), 64)]

        @pl.when((t >= 6) & (t < 2 * chunks + 6))
        def _():
            q = t - 6
            flow = q // chunks
            at_c = pl.ds(pl.multiple_of((q % chunks) * CHUNK, CHUNK), CHUNK)
            xb_copy(q).wait()
            total = pend2[q % 3] + x_recv[flow, :, at_c].astype(jnp.float32)

            @pl.when(flow == 0)
            def _():
                grad[:, at_c] = total

            @pl.when(flow == 1)
            def _():
                fwd_out[:, at_c] = (fwd_out[:, at_c].astype(jnp.float32) + total).astype(jnp.bfloat16)

        @pl.when(t == 2 * chunks - 1)
        def _():
            u_load.wait()

            def norm_back(i, carry):
                at_i = pl.ds(pl.multiple_of(i * 16, 16), 16)
                u = packed[at_i].astype(jnp.float32)
                scale = lax.rsqrt(jnp.mean(u * u, axis=1, keepdims=True) + EPSILON)
                h = grad[at_i] * gains[...]
                along = jnp.mean(h * u, axis=1, keepdims=True)
                result = scale * h - u * (scale * scale * scale * along)
                bwd_out[at_i] = (bwd_out[at_i].astype(jnp.float32) + result).astype(jnp.bfloat16)
                return carry

            lax.fori_loop(0, 4, norm_back, 0)

        return carry

    lax.fori_loop(0, 2 * chunks + 6, step, 0)


def on_device(
    fwd_in, gains, gate_weight, up_weight, down_weight, fwd_routes, fwd_probs,
    bwd_grad, bwd_input, bwd_routes, bwd_probs, bwd_stash,
):
    depth = fwd_in.shape[2]
    chunks = depth // CHUNK
    hidden = gate_weight.shape[2]
    r = np.arange(384)
    goal = np.where(r < 320, (r // 80) * 2 * CAP + r % CAP + 1000 * ((r % 80) // CAP), -1000000)
    goal = jnp.asarray(goal.reshape(1, 384), jnp.float32)
    by_y = bwd_stash[0].reshape(4, 4, 2 * CAP, 2 * hidden)
    first = jnp.stack([by_y[:, 0], by_y[:, 3]], axis=1).reshape(320, 2 * hidden)
    second = jnp.stack([by_y[:, 1], by_y[:, 2]], axis=1).reshape(320, 2 * hidden)
    stash = jnp.concatenate([first, second], axis=0)
    bf, f32 = jnp.bfloat16, jnp.float32
    vmem, hbm = pl.BlockSpec(memory_space=pltpu.VMEM), pl.BlockSpec(memory_space=pl.ANY)
    dma = pltpu.SemaphoreType.DMA
    two = 2 * chunks
    scratch = [
        pltpu.VMEM((256, 128), f32),
        pltpu.VMEM((2, 256, depth), bf),
        pltpu.VMEM((320, depth), bf),
        pltpu.VMEM((2, 320, depth), bf),
        pltpu.VMEM((2, 320, depth), bf),
        pltpu.VMEM((2, 128, depth), bf),
        pltpu.VMEM((2, 64, depth), bf),
        pltpu.VMEM((hidden, depth), bf),
        pltpu.VMEM((hidden, depth), bf),
        pltpu.VMEM((2, 2, CHUNK, hidden), bf),
        pltpu.VMEM((2, depth, hidden), bf),
        pltpu.VMEM((320, 2 * hidden), bf),
        pltpu.VMEM((320, 2 * hidden), bf),
        pltpu.VMEM((2, 2, 320, hidden), f32),
        pltpu.VMEM((2, 2, 320, hidden), bf),
        pltpu.VMEM((2, 320, hidden), bf),
        pltpu.VMEM((2, 384, 256), bf),
        pltpu.VMEM((2, 2, 256, 384), bf),
        pltpu.VMEM((3, 128, CHUNK), f32),
        pltpu.VMEM((3, 64, CHUNK), f32),
        pltpu.VMEM((64, depth), f32),
        dma((2, 2)), dma((2, 2)),
        dma((3,)), dma((3,)),
        dma((2,)), dma((2,)),
        dma((2, 3)), dma((2, 3)),
        dma((2, chunks)), dma((2, chunks)),
        dma, dma,
        dma, dma,
        dma((two, 3)), dma((two, 3)),
        dma((two,)), dma((two,)),
        dma((two,)), dma((two,)),
        dma((3,)), dma((2,)), dma((2, 2)), dma((two,)),
    ]
    fwd_result, bwd_result = pl.pallas_call(
        kernel,
        out_shape=(jax.ShapeDtypeStruct((64, depth), bf), jax.ShapeDtypeStruct((64, depth), bf)),
        in_specs=[hbm, hbm, vmem, hbm, hbm, hbm, vmem, vmem, vmem, vmem, hbm, hbm, vmem],
        out_specs=(vmem, vmem),
        scratch_shapes=scratch,
        compiler_params=pltpu.CompilerParams(
            collective_id=0, has_side_effects=True, vmem_limit_bytes=63 * 1024 * 1024
        ),
        name="routed_experts",
    )(
        fwd_in[0], bwd_grad[0], gains, gate_weight[0], up_weight[0], down_weight[0],
        fwd_routes[0], fwd_probs[0], bwd_routes[0], bwd_probs[0], bwd_input[0], stash, goal,
    )
    return (fwd_result[None], bwd_result[None])


def solution(mesh):
    rows = P("section", "expert", None)
    cols = P("section", None, "expert")
    return jax.shard_map(
        on_device,
        mesh=mesh,
        in_specs=(rows, P("section", None), cols, cols, rows, rows, rows, rows, rows, rows, rows, rows),
        out_specs=(rows, rows),
        check_vma=False,
    )
```

time: 856 us -> 341 us (0.40)
  the two profiles are of different devices: /device:TPU:29 before, /device:TPU:0 now
where the time goes in v1:
time: 341 us; the launch traced here: 339 us
  Pallas kernels  326 us (96%)
  local copies, waits for them, and re-layouts  11.8 us (3%)
    pallas_call x1, Pallas kernels, on_device(): pl.pallas_call(kernel, out_shape=(jax.ShapeDtypeStruct((64, depth), bf),...  326 us

profile of v1, /device:TPU:0, one launch (start us, length us, event | category | flops | bytes accessed | tf_op | source)
XLA Modules:
  0.0 339.3 jit_solution(14101245407846361358)
XLA Ops:
  0.6 1.4 copy.15.f_routes
  2.0 1.4 copy.16.f_probs
  3.4 1.4 copy.17.b_routes
  4.7 1.4 copy.18.b_probs
  6.1 1.0 stack.8
  7.1 1.0 fusion
  8.2 0.9 pad_maximum_fusion.stash
  9.1 325.9 %routed_experts.1 = (bf16[64,7168]{1,0:T(8,128)(2,1)}, bf16[64,7168]{1,0:T(8,128)(2,1)}) custom-call(bf16[64,7168]{1,0:T(8,128)(2,1)} %bitcast.22, bf16[64,7168]{1,0:T(8,128)(2,1)} %bitcast.23, f32[1,7168]{1,0:T(1,128)} %gains.1, bf16[7168,256]{1,0:T(8,128)(2,1)} %bitcast.15, bf16[7168,256]{1,0:T(8,128)(2,1)} %bitcast.16, bf16[256,7168]{1,0:T(8,128)(2,1)} %bitcast.17, ...), custom_call_target="tpu_custom_call" | custom-call | tf_op jit(solution)/shard_map/routed_experts/pallas_call | solution.py:458
  334.9 2.2 copy.21
  337.1 2.2 copy.22
  (1 shorter events, 0.0 us)

commit v2 on v1

v2 whole, which is shorter than its diff:
```python
import jax
import jax.numpy as jnp
import numpy as np
from jax import lax
from jax.experimental import pallas as pl
from jax.experimental.pallas import tpu as pltpu
from jax.sharding import PartitionSpec as P

EPSILON = 1e-06
MESH = pl.DeviceIdType.MESH
CAP = 20
CHUNK = 512
PARTS = 2
PIECE = 896
NT = (((1,), (1,)), ((), ()))


def mm(a, b):
    return jnp.dot(a, b, preferred_element_type=jnp.float32)


def mm_t(a, b):
    return lax.dot_general(a, b, NT, preferred_element_type=jnp.float32)


def aligned(start, size, unit):
    return pl.ds(pl.multiple_of(start, unit), size)


def slot_keys(routes, offset):
    tokens = routes.shape[0]
    lane = lax.broadcasted_iota(jnp.int32, (tokens, 128), 1)
    first, second = routes[:, 0:1], routes[:, 1:2]
    one0 = jnp.where(first == lane, 1.0, 0.0)
    one1 = jnp.where(second == lane, 1.0, 0.0)
    row = lax.broadcasted_iota(jnp.int32, (tokens, tokens), 0)
    col = lax.broadcasted_iota(jnp.int32, (tokens, tokens), 1)
    lower = jnp.where(col < row, 1.0, 0.0).astype(jnp.bfloat16)
    before = mm(lower, (one0 + one1).astype(jnp.bfloat16))
    pos0 = jnp.sum(one0 * before, axis=1, keepdims=True)
    pos1 = jnp.sum(one1 * before, axis=1, keepdims=True)
    key0 = first.astype(jnp.float32) * CAP + pos0 + offset
    key1 = second.astype(jnp.float32) * CAP + pos1 + offset
    return key0, key1


def kernel(
    fwd_in, bwd_grad, gains, wg, wu, wd, f_routes, f_probs, b_routes, b_probs, bwd_input, stash, target,
    fwd_out, bwd_out,
    meta, scale, raw, dense, packed, rows, w_own, w_peer, wd_own, wd_peer, st, acc, psend, precv, small, hid,
    irecv, ipend, back, pend, orecv, xrecv, grad, gres, pack, comb,
    relay_s, relay_r, gres_s, gres_r, scale_s, scale_r, meta_s, meta_r, o_s, o_r, z_s, z_r, i_s, i_r,
    wt_s, wt_r, wd_s, wd_r, p_s, p_r, sm_s, sm_r, hid_s, hid_r,
    ib_s, ib_r, zb_s, zb_r, ob_s, ob_r, xb_s, xb_r, loc, zloc, zbloc,
):
    depth = gains.shape[1]
    width = depth // 2
    steps = width // CHUNK
    part = width // PARTS
    hidden = wg.shape[1]
    sec = lax.axis_index("section")
    ex = lax.axis_index("expert")
    z, y, x = ex // 8, (ex // 2) % 4, ex % 2
    half = y // 2
    cls = ((y + 1) // 2) % 2
    own = aligned(half * 128, 128, 128)
    other = aligned((1 - half) * 128, 128, 128)
    mine = aligned(half * 128 + x * 64, 64, 64)
    class_own = aligned(cls * 320, 320, 320)
    class_peer = aligned((1 - cls) * 320, 320, 320)
    cols_own = aligned(x * width, width, width)
    cols_peer = aligned((1 - x) * width, width, width)
    up, down = (sec + 1) % 4, (sec + 3) % 4

    def at(zz, yy, xx):
        return zz * 8 + yy * 2 + xx

    x_peer = (sec, at(z, y, 1 - x))
    o_peer = (sec, at(z, 3 - y, x))
    d_peer = (sec, at(z, 3 - y, 1 - x))
    i_peer = (sec, at(z, y + 1 - 2 * (y % 2), x))
    z_peers = [(sec, at((z + d) % 4, y, x)) for d in (1, 2, 3)]
    relays = [(s, at(z, y, xx)) for s in (up, down) for xx in (x, 1 - x)]

    barrier = pltpu.get_barrier_semaphore()
    partners = [x_peer, o_peer, d_peer, i_peer] + z_peers + relays
    for peer in partners:
        pl.semaphore_signal(barrier, inc=1, device_id=peer, device_id_type=MESH)
    pl.semaphore_wait(barrier, len(partners))

    def remote(src, dst, send, recv, peer):
        return pltpu.make_async_remote_copy(
            src_ref=src, dst_ref=dst, send_sem=send, recv_sem=recv, device_id=peer, device_id_type=MESH
        )

    def start(copies):
        for copy in copies:
            copy.start()

    def wait(copies):
        for copy in copies:
            copy.wait()

    def cols(k):
        return pl.ds(k * part, part)

    def relay(flow, k):
        src = (bwd_grad, fwd_in)[flow]
        copies = []
        for d, xx in enumerate((x, 1 - x)):
            dst = dense.at[0, mine, cols(k)] if flow == 0 else raw.at[aligned(x * 64, 64, 64), cols(k)]
            copies.append(remote(
                src.at[:, aligned(xx * width + k * part, part, 128)], dst,
                relay_s.at[flow, k, d], relay_r.at[flow, k, d], ((down, up)[flow], at(z, y, xx)),
            ))
        return copies

    def o_copy(flow, k):
        block = dense.at[flow, own, cols(k)]
        return remote(block, block, o_s.at[flow, k], o_r.at[flow, k], o_peer)

    def z_copies(flow, k):
        return [
            remote(
                packed.at[flow, aligned(((z + d) % 4) * 80, 80, 80), cols(k)],
                rows.at[flow, aligned(cls * 320 + z * 80, 80, 80), cols(k)],
                z_s.at[flow, k, d - 1], z_r.at[flow, k, d - 1], z_peers[d - 1],
            )
            for d in (1, 2, 3)
        ]

    def z_local(flow, k):
        return pltpu.make_async_copy(
            packed.at[flow, aligned(z * 80, 80, 80), cols(k)],
            rows.at[flow, aligned(cls * 320 + z * 80, 80, 80), cols(k)], zloc.at[flow, k],
        )

    def i_copy(flow, k):
        block = rows.at[flow, class_own, cols(k)]
        return remote(block, block, i_s.at[flow, k], i_r.at[flow, k], i_peer)

    gres_copy = remote(bwd_grad.at[:, cols_peer], gres, gres_s, gres_r, (down, at(z, y, x)))
    wd_copy = remote(wd.at[:, cols_peer], wd_peer, wd_s, wd_r, x_peer)

    def w_copies(c):
        return [
            remote(
                w.at[aligned((1 - x) * width + c * CHUNK, CHUNK, CHUNK)], w_peer.at[k, aligned(c * CHUNK, CHUNK, CHUNK)],
                wt_s.at[k, c], wt_r.at[k, c], x_peer,
            )
            for k, w in enumerate((wg, wu))
        ]

    for k in range(PARTS):
        start(relay(0, k))
    loads = [
        pltpu.make_async_copy(wd.at[:, cols_own], wd_own, loc.at[0]),
        pltpu.make_async_copy(stash, st, loc.at[1]),
        pltpu.make_async_copy(wg.at[cols_own], w_own.at[0], loc.at[2]),
        pltpu.make_async_copy(wu.at[cols_own], w_own.at[1], loc.at[3]),
    ]
    start(loads)

    for i in range(4):
        v = fwd_in[pl.ds(i * 16, 16)].astype(jnp.float32)
        r = lax.rsqrt(jnp.mean(v * v, axis=1, keepdims=True) + EPSILON)
        scale[pl.ds(128 + i * 16, 16)] = jnp.broadcast_to(r, (16, 128))
    scale_copies = [
        remote(
            scale.at[pl.ds(128, 64)], scale.at[aligned(x * 64, 64, 64)],
            scale_s.at[d], scale_r.at[d], (up, at(z, y, xx)),
        )
        for d, xx in enumerate((x, 1 - x))
    ]
    start(scale_copies)
    for k in range(PARTS):
        start(relay(1, k))

    lane = lax.broadcasted_iota(jnp.int32, (64, 128), 1)
    offset = ((half * 2 + x) * 1000).astype(jnp.float32)
    columns = []
    for routes, probs in ((b_routes, b_probs), (f_routes, f_probs)):
        key0, key1 = slot_keys(routes[...], offset)
        columns += [key0, key1, probs[:, 0:1], probs[:, 1:2]]
    value = jnp.zeros((64, 128), jnp.float32)
    for i, column in enumerate(columns):
        value = jnp.where(lane == i, column, value)
    meta[mine] = value
    meta_copies = [
        remote(meta.at[mine], meta.at[mine], meta_s.at[i], meta_r.at[i], peer)
        for i, peer in enumerate((x_peer, o_peer, d_peer))
    ]
    start(meta_copies)
    wd_copy.start()
    gres_copy.start()

    def norm(k):
        def some(i, carry):
            at_i = aligned(i * 16, 16, 16)
            v = raw[at_i, cols(k)].astype(jnp.float32)
            g = gains[:, aligned(x * width + k * part, part, 128)]
            dense[1, aligned(half * 128 + i * 16, 16, 16), cols(k)] = (v * scale[at_i, 0:1] * g).astype(jnp.bfloat16)
            return carry

        lax.fori_loop(0, 8, some, 0)

    def pack_rows(flow, k):
        o_copy(flow, k).wait()
        for j in range(part // PIECE):
            at_j = pl.ds(k * part + j * PIECE, PIECE)
            packed[flow, :, at_j] = mm(pack[flow, 0:320], dense[flow, :, at_j]).astype(jnp.bfloat16)
        start(z_copies(flow, k))
        z_local(flow, k).start()

    def pass_on(flow, k):
        wait(z_copies(flow, k))
        z_local(flow, k).wait()
        i_copy(flow, k).start()

    for k in range(PARTS):
        wait(relay(0, k))
        o_copy(0, k).start()
    bwd_out[:, cols_own] = dense[0, mine]
    wait(meta_copies)
    goal = target[...] + (half * CAP).astype(jnp.float32)
    for flow in range(2):
        base = flow * 4
        one0 = jnp.where(meta[:, base : base + 1] == goal, 1.0, 0.0)
        one1 = jnp.where(meta[:, base + 1 : base + 2] == goal, 1.0, 0.0)
        pack[flow] = jnp.transpose(one0 + one1).astype(jnp.bfloat16)
        weight = one0 * meta[:, base + 2 : base + 3] + one1 * meta[:, base + 3 : base + 4]
        high = weight.astype(jnp.bfloat16)
        comb[flow, 0] = high
        comb[flow, 1] = (weight - high.astype(jnp.float32)).astype(jnp.bfloat16)
    wait(scale_copies)
    wait(relay(1, 0))
    norm(0)
    o_copy(1, 0).start()
    pack_rows(0, 0)
    wait(relay(1, 1))
    norm(1)
    o_copy(1, 1).start()
    pack_rows(0, 1)
    pass_on(0, 0)
    start(w_copies(0))
    pack_rows(1, 0)
    pass_on(0, 1)
    start(w_copies(1))
    pack_rows(1, 1)
    pass_on(1, 0)
    pass_on(1, 1)
    start(w_copies(2))

    wait(loads)
    wd_copy.wait()
    acc[...] = jnp.zeros_like(acc)
    for k in range(PARTS):
        i_copy(0, k).wait()

        def hid_grad(j, carry):
            at_j = aligned(k * part + j * PIECE, PIECE, 128)
            block = rows[0, :, at_j]
            acc[0, 0] += mm_t(block, wd_own[:, at_j])
            acc[0, 1] += mm_t(block, wd_peer[:, at_j])
            return carry

        lax.fori_loop(0, part // PIECE, hid_grad, 0)

    def p_copy(i):
        return remote(psend.at[i], precv.at[i], p_s.at[i], p_r.at[i], x_peer)

    psend[0] = acc[0, 1].astype(jnp.bfloat16)
    p_copy(0).start()
    p_copy(0).wait()

    def gates(i, carry):
        at_i = aligned(i * 160, 160, 160)
        a = st[at_i, 0:hidden].astype(jnp.float32)
        b = st[at_i, hidden : 2 * hidden].astype(jnp.float32)
        sig = jax.nn.sigmoid(a)
        g = acc[0, 0, at_i] + precv[0, at_i].astype(jnp.float32)
        small[0, 0, at_i] = (g * b * sig * (1.0 + a * (1.0 - sig))).astype(jnp.bfloat16)
        small[1, 0, at_i] = (g * a * sig).astype(jnp.bfloat16)
        return carry

    lax.fori_loop(0, 4, gates, 0)
    small_copies = [remote(small.at[k, 0], small.at[k, 1], sm_s.at[k], sm_r.at[k], x_peer) for k in range(2)]
    start(small_copies)
    start(w_copies(3))
    acc[...] = jnp.zeros_like(acc)
    wait(small_copies)
    hid_copy = remote(hid.at[0], hid.at[1], hid_s, hid_r, x_peer)

    def place(q):
        return q // steps, aligned((q % steps) * CHUNK, CHUNK, CHUNK)

    def ib_copy(q):
        flow, at_c = place(q)
        return remote(rows.at[flow, class_peer, at_c], irecv.at[flow, :, at_c], ib_s.at[q], ib_r.at[q], i_peer)

    def zb_copies(q):
        flow, at_c = place(q)
        return [
            remote(
                rows.at[flow, aligned(cls * 320 + ((z + d) % 4) * 80, 80, 80), at_c],
                back.at[flow, aligned(z * 80, 80, 80), at_c],
                zb_s.at[q, d - 1], zb_r.at[q, d - 1], z_peers[d - 1],
            )
            for d in (1, 2, 3)
        ]

    def zb_local(q):
        flow, at_c = place(q)
        return pltpu.make_async_copy(
            rows.at[flow, aligned(cls * 320 + z * 80, 80, 80), at_c],
            back.at[flow, aligned(z * 80, 80, 80), at_c], zbloc.at[q],
        )

    def ob_copy(q):
        flow, at_c = place(q)
        return remote(dense.at[flow, pl.ds(0, 128), at_c], orecv.at[flow, :, at_c], ob_s.at[q], ob_r.at[q], o_peer)

    def xb_copy(q):
        flow, at_c = place(q)
        return remote(dense.at[flow, pl.ds(128, 64), at_c], xrecv.at[flow, :, at_c], xb_s.at[q], xb_r.at[q], x_peer)

    def step(t, carry):
        at_t = aligned((t % (steps + 1)) * CHUNK, CHUNK, CHUNK)

        @pl.when(t < steps)
        def _():
            wait(w_copies(t))

            @pl.when(t + 4 < steps)
            def _():
                start(w_copies(t + 4))

            def out_grad(at_rows):
                total = mm_t(small[0, 0, at_rows], w_own[0, at_t]) + mm_t(small[1, 0, at_rows], w_own[1, at_t])
                total += mm_t(small[0, 1, at_rows], w_peer[0, at_t])
                total += mm_t(small[1, 1, at_rows], w_peer[1, at_t])
                return total

            rows[0, class_peer, at_t] = out_grad(class_peer).astype(jnp.bfloat16)
            ib_copy(t).start()
            ipend[t % 3] = out_grad(class_own)

            @pl.when(t == 0)
            def _():
                for k in range(PARTS):
                    i_copy(1, k).wait()

            block = rows[1, :, at_t]
            for k in range(2):
                acc[k, 0] += mm(block, w_own[k, at_t])
                acc[k, 1] += mm(block, w_peer[k, at_t])

            @pl.when(t == steps - 1)
            def _():
                for k in range(2):
                    psend[1 + k] = acc[k, 1].astype(jnp.bfloat16)
                    p_copy(1 + k).start()

        @pl.when(t == steps)
        def _():
            for k in range(2):
                p_copy(1 + k).wait()

            def gated(i, carry):
                at_i = aligned(i * 160, 160, 160)
                gate = acc[0, 0, at_i] + precv[1, at_i].astype(jnp.float32)
                upper = acc[1, 0, at_i] + precv[2, at_i].astype(jnp.float32)
                hid[0, at_i] = (gate * jax.nn.sigmoid(gate) * upper).astype(jnp.bfloat16)
                return carry

            lax.fori_loop(0, 4, gated, 0)
            hid_copy.start()

        @pl.when((t > steps) & (t < 2 * steps + 1))
        def _():
            @pl.when(t == steps + 1)
            def _():
                hid_copy.wait()

            def out_rows(at_rows):
                return mm(hid[0, at_rows], wd_own[:, at_t]) + mm(hid[1, at_rows], wd_peer[:, at_t])

            rows[1, class_peer, at_t] = out_rows(class_peer).astype(jnp.bfloat16)
            ib_copy(t - 1).start()
            ipend[t % 3] = out_rows(class_own)

        def lagging(lag):
            s = t - lag
            return s, s - s // (steps + 1), (s >= 0) & (s < 2 * steps + 1) & (s != steps)

        s2, q2, due2 = lagging(2)

        @pl.when(due2)
        def _():
            flow, at_c = place(q2)
            ib_copy(q2).wait()
            total = ipend[s2 % 3] + irecv[flow, :, at_c].astype(jnp.float32)
            rows[flow, class_own, at_c] = total.astype(jnp.bfloat16)
            start(zb_copies(q2))
            zb_local(q2).start()

        s4, q4, due4 = lagging(4)

        @pl.when(due4)
        def _():
            flow, at_c = place(q4)
            wait(zb_copies(q4))
            zb_local(q4).wait()
            block = back[flow, :, at_c]
            away = mm(comb[flow, 0, other, 0:320], block) + mm(comb[flow, 1, other, 0:320], block)
            dense[flow, 0:128, at_c] = away.astype(jnp.bfloat16)
            ob_copy(q4).start()
            pend[s4 % 3] = mm(comb[flow, 0, own, 0:320], block) + mm(comb[flow, 1, own, 0:320], block)

        s6, q6, due6 = lagging(6)

        @pl.when(due6)
        def _():
            flow, at_c = place(q6)
            c = (q6 % steps) * CHUNK
            rows_mine, rows_peer = aligned(x * 64, 64, 64), aligned((1 - x) * 64, 64, 64)
            ob_copy(q6).wait()
            total = pend[s6 % 3] + orecv[flow, :, at_c].astype(jnp.float32)
            at_d = aligned(x * width + c, CHUNK, CHUNK)

            @pl.when(flow == 0)
            def _():
                pend[s6 % 3] = total
                grad[:, at_d] = pend[s6 % 3, rows_mine]

            @pl.when(flow == 1)
            def _():
                pend[s6 % 3] = total + raw[:, at_c].astype(jnp.float32)
                fwd_out[:, at_d] = pend[s6 % 3, rows_mine].astype(jnp.bfloat16)

            dense[flow, 128:192, at_c] = pend[s6 % 3, rows_peer].astype(jnp.bfloat16)
            xb_copy(q6).start()

        _, q8, due8 = lagging(8)

        @pl.when(due8)
        def _():
            flow, at_c = place(q8)
            at_d = aligned((1 - x) * width + (q8 % steps) * CHUNK, CHUNK, CHUNK)
            xb_copy(q8).wait()

            @pl.when(flow == 0)
            def _():
                grad[:, at_d] = xrecv[0, :, at_c].astype(jnp.float32)

            @pl.when(flow == 1)
            def _():
                fwd_out[:, at_d] = xrecv[1, :, at_c]

        @pl.when(t == 2 * steps + 1)
        def _():
            gres_copy.wait()
            bwd_out[:, cols_peer] = gres[...]

            def norm_back(i, carry):
                at_i = aligned(i * 16, 16, 16)
                u = bwd_input[at_i].astype(jnp.float32)
                r = lax.rsqrt(jnp.mean(u * u, axis=1, keepdims=True) + EPSILON)
                h = grad[at_i] * gains[...]
                along = jnp.mean(h * u, axis=1, keepdims=True)
                result = r * h - u * (r * r * r * along)
                bwd_out[at_i] = (bwd_out[at_i].astype(jnp.float32) + result).astype(jnp.bfloat16)
                return carry

            lax.fori_loop(0, 4, norm_back, 0)

        return carry

    lax.fori_loop(0, 2 * steps + 9, step, 0)


def on_device(
    fwd_in, gains, gate_weight, up_weight, down_weight, fwd_routes, fwd_probs,
    bwd_grad, bwd_input, bwd_routes, bwd_probs, bwd_stash,
):
    depth = fwd_in.shape[2]
    width = depth // 2
    hidden = gate_weight.shape[2]
    r = np.arange(384)
    goal = np.where(r < 320, (r // 80) * 2 * CAP + r % CAP + 1000 * ((r % 80) // CAP), -1000000)
    goal = jnp.asarray(goal.reshape(1, 384), jnp.float32)
    by_y = bwd_stash[0].reshape(4, 4, 2 * CAP, 2 * hidden)
    first = jnp.stack([by_y[:, 0], by_y[:, 3]], axis=1).reshape(320, 2 * hidden)
    second = jnp.stack([by_y[:, 1], by_y[:, 2]], axis=1).reshape(320, 2 * hidden)
    stash = jnp.concatenate([first, second], axis=0)
    bf, f32 = jnp.bfloat16, jnp.float32
    vmem, hbm = pl.BlockSpec(memory_space=pltpu.VMEM), pl.BlockSpec(memory_space=pl.ANY)
    dma = pltpu.SemaphoreType.DMA
    steps = width // CHUNK
    two = 2 * steps
    scratch = [
        pltpu.VMEM((256, 128), f32),
        pltpu.VMEM((192, 128), f32),
        pltpu.VMEM((128, width), bf),
        pltpu.VMEM((2, 256, width), bf),
        pltpu.VMEM((2, 320, width), bf),
        pltpu.VMEM((2, 640, width), bf),
        pltpu.VMEM((2, width, hidden), bf),
        pltpu.VMEM((2, width, hidden), bf),
        pltpu.VMEM((hidden, width), bf),
        pltpu.VMEM((hidden, width), bf),
        pltpu.VMEM((640, 2 * hidden), bf),
        pltpu.VMEM((2, 2, 640, hidden), f32),
        pltpu.VMEM((3, 640, hidden), bf),
        pltpu.VMEM((3, 640, hidden), bf),
        pltpu.VMEM((2, 2, 640, hidden), bf),
        pltpu.VMEM((2, 640, hidden), bf),
        pltpu.VMEM((2, 320, width), bf),
        pltpu.VMEM((3, 320, CHUNK), f32),
        pltpu.VMEM((2, 320, width), bf),
        pltpu.VMEM((3, 128, CHUNK), f32),
        pltpu.VMEM((2, 128, width), bf),
        pltpu.VMEM((2, 64, width), bf),
        pltpu.VMEM((64, depth), f32),
        pltpu.VMEM((64, width), bf),
        pltpu.VMEM((2, 384, 256), bf),
        pltpu.VMEM((2, 2, 256, 384), bf),
        dma((2, PARTS, 2)), dma((2, PARTS, 2)),
        dma, dma,
        dma((2,)), dma((2,)),
        dma((3,)), dma((3,)),
        dma((2, PARTS)), dma((2, PARTS)),
        dma((2, PARTS, 3)), dma((2, PARTS, 3)),
        dma((2, PARTS)), dma((2, PARTS)),
        dma((2, steps)), dma((2, steps)),
        dma, dma,
        dma((3,)), dma((3,)),
        dma((2,)), dma((2,)),
        dma, dma,
        dma((two,)), dma((two,)),
        dma((two, 3)), dma((two, 3)),
        dma((two,)), dma((two,)),
        dma((two,)), dma((two,)),
        dma((4,)), dma((2, PARTS)), dma((two,)),
    ]
    fwd_result, bwd_result = pl.pallas_call(
        kernel,
        out_shape=(jax.ShapeDtypeStruct((64, depth), bf), jax.ShapeDtypeStruct((64, depth), bf)),
        in_specs=[vmem, hbm, vmem, hbm, hbm, hbm, vmem, vmem, vmem, vmem, vmem, hbm, vmem],
        out_specs=(vmem, vmem),
        scratch_shapes=scratch,
        compiler_params=pltpu.CompilerParams(
            collective_id=0, has_side_effects=True, vmem_limit_bytes=63 * 1024 * 1024
        ),
        name="routed_experts",
    )(
        fwd_in[0], bwd_grad[0], gains, gate_weight[0], up_weight[0], down_weight[0],
        fwd_routes[0], fwd_probs[0], bwd_routes[0], bwd_probs[0], bwd_input[0], stash, goal,
    )
    return (fwd_result[None], bwd_result[None])


def solution(mesh):
    rows = P("section", "expert", None)
    cols = P("section", None, "expert")
    return jax.shard_map(
        on_device,
        mesh=mesh,
        in_specs=(rows, P("section", None), cols, cols, rows, rows, rows, rows, rows, rows, rows, rows),
        out_specs=(rows, rows),
        check_vma=False,
    )
```

time: 341 us -> 280 us (0.82)
  Pallas kernels: 326 us -> 265 us
    pallas_call x1, Pallas kernels: 326 us -> 265 us  [on_device(): pl.pallas_call(kernel, out_shape=(jax.ShapeDtypeStruct((64, depth), bf),...]
where the time goes in v2:
time: 280 us; the launch traced here: 279 us
  Pallas kernels  265 us (95%)
  local copies, waits for them, and re-layouts  11.8 us (4%)
    pallas_call x1, Pallas kernels, on_device(): pl.pallas_call(kernel, out_shape=(jax.ShapeDtypeStruct((64, depth), bf),...  265 us

profile of v2, /device:TPU:0, one launch (start us, length us, event | category | flops | bytes accessed | tf_op | source)
XLA Modules:
  0.0 278.9 jit_solution(3203875726653077852)
XLA Ops:
  0.6 1.4 copy.15.f_routes
  2.0 1.4 copy.16.f_probs
  3.4 1.4 copy.17.b_routes
  4.7 1.4 copy.18.b_probs
  6.1 1.0 stack.8
  7.1 1.0 fusion
  8.2 0.9 pad_maximum_fusion.stash
  9.1 265.5 %routed_experts.1 = (bf16[64,7168]{1,0:T(8,128)(2,1)}, bf16[64,7168]{1,0:T(8,128)(2,1)}) custom-call(bf16[64,7168]{1,0:T(8,128)(2,1)} %bitcast.22, bf16[64,7168]{1,0:T(8,128)(2,1)} %bitcast.23, f32[1,7168]{1,0:T(1,128)} %gains.1, bf16[7168,256]{1,0:T(8,128)(2,1)} %bitcast.15, bf16[7168,256]{1,0:T(8,128)(2,1)} %bitcast.16, bf16[256,7168]{1,0:T(8,128)(2,1)} %bitcast.17, ...), custom_call_target="tpu_custom_call" | custom-call | tf_op jit(solution)/shard_map/routed_experts/pallas_call | solution.py:546
  274.5 2.2 copy.21
  276.7 2.2 copy.22
  (1 shorter events, 0.0 us)

commit v3 on v2

v3 whole, which is shorter than its diff:
```python
import jax
import jax.numpy as jnp
import numpy as np
from jax import lax
from jax.experimental import pallas as pl
from jax.experimental.pallas import tpu as pltpu
from jax.sharding import PartitionSpec as P

EPSILON = 1e-06
MESH = pl.DeviceIdType.MESH
CAP = 20
EARLY = 4
RING = 4
CHUNK = 512
PARTS = 4
PIECE = 896
NT = (((1,), (1,)), ((), ()))


def mm(a, b):
    return jnp.dot(a, b, preferred_element_type=jnp.float32)


def mm_t(a, b):
    return lax.dot_general(a, b, NT, preferred_element_type=jnp.float32)


def aligned(start, size, unit):
    return pl.ds(pl.multiple_of(start, unit), size)


def slot_keys(first, second, offset):
    tokens = first.shape[1]
    expert = lax.broadcasted_iota(jnp.int32, (8, tokens), 0).astype(jnp.float32)
    one0 = jnp.where(first == expert, 1.0, 0.0)
    one1 = jnp.where(second == expert, 1.0, 0.0)
    row = lax.broadcasted_iota(jnp.int32, (tokens, tokens), 0)
    col = lax.broadcasted_iota(jnp.int32, (tokens, tokens), 1)
    earlier = jnp.where(row < col, 1.0, 0.0).astype(jnp.bfloat16)
    before = mm((one0 + one1).astype(jnp.bfloat16), earlier)
    pos0 = jnp.sum(one0 * before, axis=0, keepdims=True)
    pos1 = jnp.sum(one1 * before, axis=0, keepdims=True)
    return first * CAP + pos0 + offset, second * CAP + pos1 + offset


def kernel(
    fwd_in, bwd_grad, gains, wg, wu, wd, f_routes, f_probs, b_routes, b_probs, bwd_input, stash, target,
    fwd_out, bwd_out,
    told, meta, scales, scale, raw, dense, packed, rows, w_own, w_peer, wd_own, wd_peer, st, acc, psend, precv, small, hid,
    irecv, ipend, back, back2, pend, pend2, orecv, orecv2, xrecv, grad, gres, pack, comb,
    relay_s, relay_r, gres_s, gres_r, scale_s, scale_r, meta_s, meta_r, o_s, o_r, z_s, z_r, i_s, i_r,
    wt_s, wt_r, wd_s, wd_r, p_s, p_r, sm_s, sm_r, hid_s, hid_r,
    ib_s, ib_r, zz_s, zz_r, zzloc, zb_s, zb_r, ob_s, ob_r, xb_s, xb_r, loc, zloc, zbloc,
):
    depth = gains.shape[1]
    width = depth // 2
    steps = width // CHUNK
    part = width // PARTS
    hidden = wg.shape[1]
    sec = lax.axis_index("section")
    ex = lax.axis_index("expert")
    z, y, x = ex // 8, (ex // 2) % 4, ex % 2
    half = y // 2
    cls = ((y + 1) // 2) % 2
    own = aligned(half * 128, 128, 128)
    other = aligned((1 - half) * 128, 128, 128)
    mine = aligned(half * 128 + x * 64, 64, 64)
    class_own = aligned(cls * 320, 320, 320)
    class_peer = aligned((1 - cls) * 320, 320, 320)
    cols_own = aligned(x * width, width, width)
    cols_peer = aligned((1 - x) * width, width, width)
    up, down = (sec + 1) % 4, (sec + 3) % 4

    def at(zz, yy, xx):
        return zz * 8 + yy * 2 + xx

    x_peer = (sec, at(z, y, 1 - x))
    o_peer = (sec, at(z, 3 - y, x))
    d_peer = (sec, at(z, 3 - y, 1 - x))
    i_peer = (sec, at(z, y + 1 - 2 * (y % 2), x))
    c_peers = [(sec, at(z, yy, xx)) for yy in (y + 1 - 2 * (y % 2), 2 + y % 2 - 2 * half) for xx in (x, 1 - x)]
    z_peers = [(sec, at((z + d) % 4, y, x)) for d in (1, 2, 3)]
    relays = [(s, at(z, y, xx)) for s in (up, down) for xx in (x, 1 - x)]

    barrier = pltpu.get_barrier_semaphore()
    partners = [x_peer, o_peer, d_peer] + c_peers + z_peers + relays
    for peer in partners:
        pl.semaphore_signal(barrier, inc=1, device_id=peer, device_id_type=MESH)
    pl.semaphore_wait(barrier, len(partners))

    def remote(src, dst, send, recv, peer):
        return pltpu.make_async_remote_copy(
            src_ref=src, dst_ref=dst, send_sem=send, recv_sem=recv, device_id=peer, device_id_type=MESH
        )

    def start(copies):
        for copy in copies:
            copy.start()

    def wait(copies):
        for copy in copies:
            copy.wait()

    def cols(k):
        return pl.ds(k * part, part)

    def relay(flow, k):
        src = (bwd_grad, fwd_in)[flow]
        copies = []
        for d, xx in enumerate((x, 1 - x)):
            dst = dense.at[0, mine, cols(k)] if flow == 0 else raw.at[aligned(x * 64, 64, 64), cols(k)]
            copies.append(remote(
                src.at[:, aligned(xx * width + k * part, part, 128)], dst,
                relay_s.at[flow, k, d], relay_r.at[flow, k, d], ((down, up)[flow], at(z, y, xx)),
            ))
        return copies

    def o_copy(flow, k):
        block = dense.at[flow, own, cols(k)]
        return remote(block, block, o_s.at[flow, k], o_r.at[flow, k], o_peer)

    def z_copies(flow, k):
        return [
            remote(
                packed.at[flow, aligned(((z + d) % 4) * 80, 80, 80), cols(k)],
                rows.at[flow, aligned(cls * 320 + z * 80, 80, 80), cols(k)],
                z_s.at[flow, k, d - 1], z_r.at[flow, k, d - 1], z_peers[d - 1],
            )
            for d in (1, 2, 3)
        ]

    def z_local(flow, k):
        return pltpu.make_async_copy(
            packed.at[flow, aligned(z * 80, 80, 80), cols(k)],
            rows.at[flow, aligned(cls * 320 + z * 80, 80, 80), cols(k)], zloc.at[flow, k],
        )

    def i_copy(flow, k):
        block = rows.at[flow, class_own, cols(k)]
        return remote(block, block, i_s.at[flow, k], i_r.at[flow, k], i_peer)

    gres_copy = remote(bwd_grad.at[:, cols_peer], gres, gres_s, gres_r, (down, at(z, y, x)))
    wd_copy = remote(wd.at[:, cols_peer], wd_peer, wd_s, wd_r, x_peer)

    def w_copies(c):
        return [
            remote(
                w.at[aligned((1 - x) * width + c * CHUNK, CHUNK, CHUNK)], w_peer.at[k, aligned(c * CHUNK, CHUNK, CHUNK)],
                wt_s.at[k, c], wt_r.at[k, c], x_peer,
            )
            for k, w in enumerate((wg, wu))
        ]

    for k in range(PARTS):
        start(relay(0, k))
    loads = [
        pltpu.make_async_copy(wd.at[:, cols_own], wd_own, loc.at[0]),
        pltpu.make_async_copy(stash.at[:, 0:hidden], small.at[0, 0], loc.at[1]),
        pltpu.make_async_copy(stash.at[:, hidden : 2 * hidden], small.at[1, 0], loc.at[4]),
        pltpu.make_async_copy(wg.at[cols_own], w_own.at[0], loc.at[2]),
        pltpu.make_async_copy(wu.at[cols_own], w_own.at[1], loc.at[3]),
    ]
    start(loads)

    offset = ((half * 2 + x) * 1000).astype(jnp.float32)
    lines = []
    for routes, probs in ((b_routes, b_probs), (f_routes, f_probs)):
        chosen = routes[...].astype(jnp.float32)
        lines += [*slot_keys(chosen[0:1], chosen[1:2], offset), probs[...]]
    lines = jnp.concatenate(lines, axis=0)
    my_lines = aligned((cls * 4 + half * 2 + x) * 8, 8, 8)
    told[my_lines] = jnp.concatenate([lines, jnp.zeros((8, 64), jnp.float32)], axis=1)
    meta_copies = [
        remote(told.at[my_lines], told.at[my_lines], meta_s.at[i], meta_r.at[i], peer)
        for i, peer in enumerate([x_peer, o_peer, d_peer] + c_peers)
    ]
    start(meta_copies)

    for i in range(4):
        v = fwd_in[pl.ds(i * 16, 16)].astype(jnp.float32)
        r = lax.rsqrt(jnp.mean(v * v, axis=1, keepdims=True) + EPSILON)
        scale[pl.ds(i * 16, 16)] = jnp.broadcast_to(r, (16, 128))
    turned = jnp.transpose(jnp.concatenate([scale[0:64], jnp.zeros((64, 128), jnp.float32)], axis=0))
    scales[16:24] = turned[0:8]
    scale_copies = [
        remote(
            scales.at[16:24], scales.at[aligned(x * 8, 8, 8)], scale_s.at[d], scale_r.at[d], (up, at(z, y, xx))
        )
        for d, xx in enumerate((x, 1 - x))
    ]
    start(scale_copies)
    for k in range(PARTS):
        start(relay(1, k))
    wd_copy.start()

    def norm(k):
        def some(i, carry):
            at_i = aligned(i * 16, 16, 16)
            v = raw[at_i, cols(k)].astype(jnp.float32)
            g = gains[:, aligned(x * width + k * part, part, 128)]
            dense[1, aligned(half * 128 + i * 16, 16, 16), cols(k)] = (v * scale[at_i, 0:1] * g).astype(jnp.bfloat16)
            return carry

        lax.fori_loop(0, 8, some, 0)

    def pack_rows(flow, k):
        o_copy(flow, k).wait()
        for j in range(part // PIECE):
            at_j = pl.ds(k * part + j * PIECE, PIECE)
            packed[flow, :, at_j] = mm(pack[flow, 0:320], dense[flow, :, at_j]).astype(jnp.bfloat16)
        start(z_copies(flow, k))
        z_local(flow, k).start()

    def pass_on(flow, k):
        wait(z_copies(flow, k))
        z_local(flow, k).wait()
        i_copy(flow, k).start()

    def relayed(flow, k):
        wait(relay(flow, k))
        if flow == 1:
            norm(k)
        o_copy(flow, k).start()

    goal = target[...] + (half * CAP).astype(jnp.float32)

    def column(group, i):
        return meta[aligned(group * 256, 256, 256), i : i + 1]

    def matches(group, i):
        return jnp.where(column(group, i) == goal, 1.0, 0.0)

    def build_pack(flow):
        pack[flow] = jnp.transpose(matches(cls, flow * 4) + matches(cls, flow * 4 + 1)).astype(jnp.bfloat16)

    def build_comb(at_i, group, base):
        weight = matches(group, base) * column(group, base + 2) + matches(group, base + 1) * column(group, base + 3)
        high = weight.astype(jnp.bfloat16)
        comb[at_i, 0] = high
        comb[at_i, 1] = (weight - high.astype(jnp.float32)).astype(jnp.bfloat16)

    relayed(0, 0)
    relayed(0, 1)
    wait(meta_copies)
    turned = jnp.transpose(jnp.concatenate([told[...], jnp.zeros((64, 128), jnp.float32)], axis=0))
    for i in range(8):
        meta[i * 64 : i * 64 + 64, 0:8] = turned[0:64, i * 8 : i * 8 + 8]
    build_pack(0)
    relayed(0, 2)
    pack_rows(0, 0)
    relayed(0, 3)
    pack_rows(0, 1)
    wait(scale_copies)
    both = jnp.concatenate([scales[0:1, 0:64], scales[8:9, 0:64]], axis=1)
    scale[...] = jnp.transpose(jnp.broadcast_to(both, (128, 128)))
    relayed(1, 0)
    pass_on(0, 0)
    pack_rows(0, 2)
    relayed(1, 1)
    pass_on(0, 1)
    pack_rows(0, 3)
    relayed(1, 2)
    build_pack(1)
    pass_on(0, 2)
    relayed(1, 3)
    start(w_copies(0))
    pass_on(0, 3)
    pack_rows(1, 0)
    pack_rows(1, 1)
    start(w_copies(1))
    pack_rows(1, 2)
    pass_on(1, 0)
    pack_rows(1, 3)
    pass_on(1, 1)
    start(w_copies(2))
    pass_on(1, 2)
    pass_on(1, 3)
    bwd_out[:, cols_own] = dense[0, mine]
    build_comb(0, cls, 0)
    build_comb(1, cls, 4)
    build_comb(2, 1 - cls, 4)
    wait(loads)
    for c, pair in enumerate(((0, 3), (1, 2))):
        for zz in range(4):
            for k in range(2):
                blocks = [small[k, 0, zz * 160 + yy * 40 : zz * 160 + yy * 40 + 40].astype(jnp.float32) for yy in pair]
                at_block = pl.ds(c * 320 + zz * 80, 80)
                st[at_block, k * hidden : (k + 1) * hidden] = jnp.concatenate(blocks, axis=0).astype(jnp.bfloat16)
    u_loads = [
        pltpu.make_async_copy(
            bwd_input.at[:, pl.ds(k * width, width)], packed.at[0, pl.ds(128 + k * 64, 64)], loc.at[5 + k]
        )
        for k in range(2)
    ]
    start(u_loads)

    wd_copy.wait()
    acc[...] = jnp.zeros_like(acc)
    for k in range(PARTS):
        i_copy(0, k).wait()

        def hid_grad(j, carry):
            at_j = aligned(k * part + j * PIECE, PIECE, 128)
            block = rows[0, :, at_j]
            acc[0, 0] += mm_t(block, wd_own[:, at_j])
            acc[0, 1] += mm_t(block, wd_peer[:, at_j])
            return carry

        lax.fori_loop(0, part // PIECE, hid_grad, 0)

    classes = (class_peer, class_own)

    def p_copy(i, h):
        return remote(psend.at[i, classes[h]], precv.at[i, classes[h]], p_s.at[i, h], p_r.at[i, h], x_peer)

    psend[0] = acc[0, 1].astype(jnp.bfloat16)
    for h in range(2):
        p_copy(0, h).start()
    for h in range(2):
        p_copy(0, h).wait()

    def gates(i, carry):
        at_i = aligned(i * 160, 160, 160)
        a = st[at_i, 0:hidden].astype(jnp.float32)
        b = st[at_i, hidden : 2 * hidden].astype(jnp.float32)
        sig = jax.nn.sigmoid(a)
        g = acc[0, 0, at_i] + precv[0, at_i].astype(jnp.float32)
        small[0, 0, at_i] = (g * b * sig * (1.0 + a * (1.0 - sig))).astype(jnp.bfloat16)
        small[1, 0, at_i] = (g * a * sig).astype(jnp.bfloat16)
        return carry

    lax.fori_loop(0, 4, gates, 0)
    small_copies = [remote(small.at[k, 0], small.at[k, 1], sm_s.at[k], sm_r.at[k], x_peer) for k in range(2)]
    start(small_copies)
    start(w_copies(3))
    acc[...] = jnp.zeros_like(acc)
    wait(small_copies)

    def hid_copy(h):
        return remote(hid.at[0, classes[h]], hid.at[1, classes[h]], hid_s.at[h], hid_r.at[h], x_peer)


    def plain(q):
        return (q < steps) | ((q - steps) % 2 == 0)

    def place(q):
        return q // steps, aligned((q % steps) * CHUNK, CHUNK, CHUNK)

    def ib_copy(q):
        flow, at_c = place(q)
        return remote(rows.at[flow, class_peer, at_c], irecv.at[flow, :, at_c], ib_s.at[q], ib_r.at[q], i_peer)

    def zb_copies(q):
        flow, at_c = place(q)
        return [
            remote(
                rows.at[flow, aligned(cls * 320 + ((z + d) % 4) * 80, 80, 80), at_c],
                back.at[flow, aligned(z * 80, 80, 80), at_c],
                zb_s.at[q, d - 1], zb_r.at[q, d - 1], z_peers[d - 1],
            )
            for d in (1, 2, 3)
        ]

    def zb_local(q):
        flow, at_c = place(q)
        return pltpu.make_async_copy(
            rows.at[flow, aligned(cls * 320 + z * 80, 80, 80), at_c],
            back.at[flow, aligned(z * 80, 80, 80), at_c], zbloc.at[q],
        )

    def ob_copy(q):
        flow, at_c = place(q)
        return remote(dense.at[flow, pl.ds(0, 128), at_c], orecv.at[flow, :, at_c], ob_s.at[q], ob_r.at[q], o_peer)

    def xb_copy(q):
        flow, at_c = place(q)
        return remote(dense.at[flow, pl.ds(128, 64), at_c], xrecv.at[flow, :, at_c], xb_s.at[q], xb_r.at[q], x_peer)

    def gate_sums(c):
        at_c = aligned(c * CHUNK, CHUNK, CHUNK)
        block = rows[1, :, at_c]
        for k in range(2):
            acc[k, 0] += mm(block, w_own[k, at_c])
            acc[k, 1] += mm(block, w_peer[k, at_c])

    def out_grad(c, carry):
        at_c = aligned(c * CHUNK, CHUNK, CHUNK)
        wait(w_copies(c))

        @pl.when(c + 4 < steps)
        def _():
            start(w_copies(c + 4))

        def total(at_rows):
            value = mm_t(small[0, 0, at_rows], w_own[0, at_c]) + mm_t(small[1, 0, at_rows], w_own[1, at_c])
            value += mm_t(small[0, 1, at_rows], w_peer[0, at_c])
            value += mm_t(small[1, 1, at_rows], w_peer[1, at_c])
            return value

        rows[0, class_peer, at_c] = total(class_peer).astype(jnp.bfloat16)
        ib_copy(c).start()
        ipend[c] = total(class_own)

        @pl.when(c == EARLY)
        def _():
            for k in range(PARTS):
                i_copy(1, k).wait()

            def earlier(j, carry):
                gate_sums(j)
                return carry

            lax.fori_loop(0, EARLY, earlier, 0)

        @pl.when(c >= EARLY)
        def _():
            gate_sums(c)

        return carry

    def out_rows(c):
        at_c = aligned(c * CHUNK, CHUNK, CHUNK)

        def total(at_rows):
            return mm(hid[0, at_rows], wd_own[:, at_c]) + mm(hid[1, at_rows], wd_peer[:, at_c])

        rows[1, class_peer, at_c] = total(class_peer).astype(jnp.bfloat16)

        @pl.when(c % 2 == 0)
        def _():
            ib_copy(steps + c).start()

        @pl.when(c % 2 == 1)
        def _():
            for j in range(3):
                zz_copy(c // 2, 0, j).start()
            zz_local(c // 2, 0).start()

        @pl.when(c == 0)
        def _():
            hid_copy(1).wait()

        @pl.when(c % 2 == 0)
        def _():
            ipend[c] = total(class_own)

        @pl.when(c % 2 == 1)
        def _():
            rows[1, class_own, at_c] = total(class_own).astype(jnp.bfloat16)
            for j in range(3):
                zz_copy(c // 2, 1, j).start()
            zz_local(c // 2, 1).start()

    def zz_copy(b, h, j):
        at_c = aligned((2 * b + 1) * CHUNK, CHUNK, CHUNK)
        src_row = ((1 - cls) if h == 0 else cls) * 320 + ((z + j + 1) % 4) * 80
        at_z = aligned(z * 80, 80, 80)
        dst = back2.at[at_z, aligned(b * CHUNK, CHUNK, CHUNK)] if h == 0 else back.at[1, at_z, at_c]
        return remote(
            rows.at[1, aligned(src_row, 80, 80), at_c], dst, zz_s.at[b, h, j], zz_r.at[b, h, j], z_peers[j]
        )

    def zz_local(b, h):
        at_c = aligned((2 * b + 1) * CHUNK, CHUNK, CHUNK)
        src_row = ((1 - cls) if h == 0 else cls) * 320 + z * 80
        at_z = aligned(z * 80, 80, 80)
        dst = back2.at[at_z, aligned(b * CHUNK, CHUNK, CHUNK)] if h == 0 else back.at[1, at_z, at_c]
        return pltpu.make_async_copy(rows.at[1, aligned(src_row, 80, 80), at_c], dst, zzloc.at[b, h])

    def oo_copy(q):
        _, at_c = place(q)
        b = (q - steps) // 2
        return remote(
            packed.at[1, pl.ds(0, 256), at_c], orecv2.at[:, aligned(b * CHUNK, CHUNK, CHUNK)],
            ob_s.at[q], ob_r.at[q], o_peer,
        )

    def ii_copy(q):
        _, at_c = place(q)
        return remote(packed.at[0, pl.ds(0, 128), at_c], irecv.at[1, pl.ds(0, 128), at_c], ib_s.at[q], ib_r.at[q], i_peer)

    def combine_all(q):
        _, at_c = place(q)
        b = (q - steps) // 2
        for h in range(2):
            for j in range(3):
                zz_copy(b, h, j).wait()
            zz_local(b, h).wait()
            i = 2 - h
            block = back2[:, aligned(b * CHUNK, CHUNK, CHUNK)] if h == 0 else back[1, :, at_c]
            away = mm(comb[i, 0, other, 0:320], block) + mm(comb[i, 1, other, 0:320], block)
            at_group = aligned(((1 - cls) if h == 0 else cls) * 128, 128, 128)
            packed[1, at_group, at_c] = away.astype(jnp.bfloat16)
            pend2[b % 2, h] = mm(comb[i, 0, own, 0:320], block) + mm(comb[i, 1, own, 0:320], block)
        oo_copy(q).start()

    def add_outer_all(q):
        _, at_c = place(q)
        b = (q - steps) // 2
        at_b = aligned(b * CHUNK, CHUNK, CHUNK)
        oo_copy(q).wait()
        peers = pend2[b % 2, 0] + orecv2[aligned((1 - cls) * 128, 128, 128), at_b].astype(jnp.float32)
        packed[0, 0:128, at_c] = peers.astype(jnp.bfloat16)
        ii_copy(q).start()
        pend[q % RING] = pend2[b % 2, 1] + orecv2[aligned(cls * 128, 128, 128), at_b].astype(jnp.float32)

    def add_pair(q):
        flow, at_c = place(q)
        ib_copy(q).wait()
        total = ipend[q % steps] + irecv[flow, :, at_c].astype(jnp.float32)
        rows[flow, class_own, at_c] = total.astype(jnp.bfloat16)
        start(zb_copies(q))
        zb_local(q).start()

    def combine(q):
        flow, at_c = place(q)
        wait(zb_copies(q))
        zb_local(q).wait()
        block = back[flow, :, at_c]
        away = mm(comb[flow, 0, other, 0:320], block) + mm(comb[flow, 1, other, 0:320], block)
        dense[flow, 0:128, at_c] = away.astype(jnp.bfloat16)
        ob_copy(q).start()
        pend[q % RING] = mm(comb[flow, 0, own, 0:320], block) + mm(comb[flow, 1, own, 0:320], block)

    def add_outer(q):
        flow, at_c = place(q)
        slot = q % RING
        rows_mine, rows_peer = aligned(x * 64, 64, 64), aligned((1 - x) * 64, 64, 64)

        @pl.when(plain(q))
        def _():
            ob_copy(q).wait()
            pend[slot] += orecv[flow, :, at_c].astype(jnp.float32)

        @pl.when(jnp.logical_not(plain(q)))
        def _():
            ii_copy(q).wait()
            pend[slot] += irecv[1, 0:128, at_c].astype(jnp.float32)

        at_d = aligned(x * width + (q % steps) * CHUNK, CHUNK, CHUNK)

        @pl.when(flow == 0)
        def _():
            grad[:, at_d] = pend[slot, rows_mine]

        @pl.when(flow == 1)
        def _():
            pend[slot] += raw[:, at_c].astype(jnp.float32)
            fwd_out[:, at_d] = pend[slot, rows_mine].astype(jnp.bfloat16)

        dense[flow, 128:192, at_c] = pend[slot, rows_peer].astype(jnp.bfloat16)
        xb_copy(q).start()

    def finish(q):
        flow, at_c = place(q)
        at_d = aligned((1 - x) * width + (q % steps) * CHUNK, CHUNK, CHUNK)
        xb_copy(q).wait()

        @pl.when(flow == 0)
        def _():
            grad[:, at_d] = xrecv[0, :, at_c].astype(jnp.float32)

        @pl.when(flow == 1)
        def _():
            fwd_out[:, at_d] = xrecv[1, :, at_c]

    def each(first, last, stage):
        def one(q, carry):
            stage(q)
            return carry

        lax.fori_loop(first, last, one, 0)

    lax.fori_loop(0, steps, out_grad, 0)
    for h in range(2):
        for k in range(2):
            psend[1 + k, classes[h]] = acc[k, 1, classes[h]].astype(jnp.bfloat16)
            p_copy(1 + k, h).start()
    each(0, 2, add_pair)

    def gated(h):
        for k in range(2):
            p_copy(1 + k, h).wait()

        def some(i, carry):
            start_row = (1 - cls if h == 0 else cls) * 320
            at_i = aligned(start_row + i * 160, 160, 160)
            gate = acc[0, 0, at_i] + precv[1, at_i].astype(jnp.float32)
            upper = acc[1, 0, at_i] + precv[2, at_i].astype(jnp.float32)
            hid[0, at_i] = (gate * jax.nn.sigmoid(gate) * upper).astype(jnp.bfloat16)
            return carry

        lax.fori_loop(0, 2, some, 0)
        hid_copy(h).start()

    gated(0)
    each(2, 4, add_pair)
    gated(1)
    gres_copy.start()
    each(4, 5, add_pair)
    hid_copy(0).wait()

    def step(t, carry):
        @pl.when(t < steps)
        def _():
            out_rows(t)

        def stage(q, least, do):
            @pl.when((q >= least) & (q < 2 * steps))
            def _():
                do(q)

        def two_ways(q, least, do, do_odd):
            @pl.when((q >= least) & (q < 2 * steps) & plain(q))
            def _():
                do(q)

            @pl.when((q >= steps) & (q < 2 * steps) & jnp.logical_not(plain(q)))
            def _():
                do_odd(q)

        two_ways(t + 5, 5, add_pair, combine_all)

        @pl.when(t == 0)
        def _():
            each(0, 3, combine)
            add_outer(0)

        two_ways(t + 3, 3, combine, add_outer_all)
        stage(t + 1, 1, add_outer)
        stage(t - 1, 0, finish)

        @pl.when(t == steps + 1)
        def _():
            wait(u_loads)
            gres_copy.wait()
            bwd_out[:, cols_peer] = gres[...]

            def norm_back(i, carry):
                at_i = aligned(i * 16, 16, 16)
                at_u = [aligned(128 + k * 64 + i * 16, 16, 16) for k in range(2)]
                u = jnp.concatenate([packed[0, at_k] for at_k in at_u], axis=1).astype(jnp.float32)
                r = lax.rsqrt(jnp.mean(u * u, axis=1, keepdims=True) + EPSILON)
                h = grad[at_i] * gains[...]
                along = jnp.mean(h * u, axis=1, keepdims=True)
                result = r * h - u * (r * r * r * along)
                bwd_out[at_i] = (bwd_out[at_i].astype(jnp.float32) + result).astype(jnp.bfloat16)
                return carry

            lax.fori_loop(0, 4, norm_back, 0)

        return carry

    lax.fori_loop(0, 2 * steps + 1, step, 0)


def on_device(
    fwd_in, gains, gate_weight, up_weight, down_weight, fwd_routes, fwd_probs,
    bwd_grad, bwd_input, bwd_routes, bwd_probs, bwd_stash,
):
    depth = fwd_in.shape[2]
    width = depth // 2
    hidden = gate_weight.shape[2]
    r = np.arange(384)
    goal = np.where(r < 320, (r // 80) * 2 * CAP + r % CAP + 1000 * ((r % 80) // CAP), -1000000)
    goal = jnp.asarray(goal.reshape(1, 384), jnp.float32)
    bf, f32 = jnp.bfloat16, jnp.float32
    vmem, hbm = pl.BlockSpec(memory_space=pltpu.VMEM), pl.BlockSpec(memory_space=pl.ANY)
    dma = pltpu.SemaphoreType.DMA
    steps = width // CHUNK
    two = 2 * steps
    scratch = [
        pltpu.VMEM((64, 128), f32),
        pltpu.VMEM((512, 128), f32),
        pltpu.VMEM((24, 128), f32),
        pltpu.VMEM((128, 128), f32),
        pltpu.VMEM((128, width), bf),
        pltpu.VMEM((2, 256, width), bf),
        pltpu.VMEM((2, 320, width), bf),
        pltpu.VMEM((2, 640, width), bf),
        pltpu.VMEM((2, width, hidden), bf),
        pltpu.VMEM((2, width, hidden), bf),
        pltpu.VMEM((hidden, width), bf),
        pltpu.VMEM((hidden, width), bf),
        pltpu.VMEM((640, 2 * hidden), bf),
        pltpu.VMEM((2, 2, 640, hidden), f32),
        pltpu.VMEM((3, 640, hidden), bf),
        pltpu.VMEM((3, 640, hidden), bf),
        pltpu.VMEM((2, 2, 640, hidden), bf),
        pltpu.VMEM((2, 640, hidden), bf),
        pltpu.VMEM((2, 320, width), bf),
        pltpu.VMEM((steps, 320, CHUNK), f32),
        pltpu.VMEM((2, 320, width), bf),
        pltpu.VMEM((320, steps // 2 * CHUNK), bf),
        pltpu.VMEM((RING, 128, CHUNK), f32),
        pltpu.VMEM((2, 2, 128, CHUNK), f32),
        pltpu.VMEM((2, 128, width), bf),
        pltpu.VMEM((256, steps // 2 * CHUNK), bf),
        pltpu.VMEM((2, 64, width), bf),
        pltpu.VMEM((64, depth), f32),
        pltpu.VMEM((64, width), bf),
        pltpu.VMEM((2, 384, 256), bf),
        pltpu.VMEM((3, 2, 256, 384), bf),
        dma((2, PARTS, 2)), dma((2, PARTS, 2)),
        dma, dma,
        dma((2,)), dma((2,)),
        dma((7,)), dma((7,)),
        dma((2, PARTS)), dma((2, PARTS)),
        dma((2, PARTS, 3)), dma((2, PARTS, 3)),
        dma((2, PARTS)), dma((2, PARTS)),
        dma((2, steps)), dma((2, steps)),
        dma, dma,
        dma((3, 2)), dma((3, 2)),
        dma((2,)), dma((2,)),
        dma((2,)), dma((2,)),
        dma((two,)), dma((two,)),
        dma((steps // 2, 2, 3)), dma((steps // 2, 2, 3)), dma((steps // 2, 2)),
        dma((two, 3)), dma((two, 3)),
        dma((two,)), dma((two,)),
        dma((two,)), dma((two,)),
        dma((7,)), dma((2, PARTS)), dma((two,)),
    ]
    fwd_result, bwd_result = pl.pallas_call(
        kernel,
        out_shape=(jax.ShapeDtypeStruct((64, depth), bf), jax.ShapeDtypeStruct((64, depth), bf)),
        in_specs=[vmem, hbm, vmem, hbm, hbm, hbm, vmem, vmem, vmem, vmem, hbm, hbm, vmem],
        out_specs=(vmem, vmem),
        scratch_shapes=scratch,
        compiler_params=pltpu.CompilerParams(
            collective_id=0, has_side_effects=True, vmem_limit_bytes=63 * 1024 * 1024
        ),
        name="routed_experts",
    )(
        fwd_in[0], bwd_grad[0], gains, gate_weight[0], up_weight[0], down_weight[0],
        fwd_routes[0].T, fwd_probs[0].T, bwd_routes[0].T, bwd_probs[0].T, bwd_input[0], bwd_stash[0], goal,
    )
    return (fwd_result[None], bwd_result[None])


def solution(mesh):
    rows = P("section", "expert", None)
    cols = P("section", None, "expert")
    return jax.shard_map(
        on_device,
        mesh=mesh,
        in_specs=(rows, P("section", None), cols, cols, rows, rows, rows, rows, rows, rows, rows, rows),
        out_specs=(rows, rows),
        check_vma=False,
    )
```

time: 280 us -> 264 us (0.943)
  local copies, waits for them, and re-layouts: 11.8 us -> 4.32 us
  Pallas kernels: 265 us -> 259 us
    pallas_call x1, Pallas kernels: 265 us -> 259 us  [on_device(): pl.pallas_call(kernel, out_shape=(jax.ShapeDtypeStruct((64, depth), bf),...]
    squeeze x4 -> x0, local copies, waits for them, and re-layouts: 5.49 us -> none  [the longest x1 1.38 us: on_device(): fwd_routes[0]]
where the time goes in v3:
time: 264 us
  Pallas kernels  259 us (98%)
  local copies, waits for them, and re-layouts  4.32 us (2%)
    pallas_call x1, Pallas kernels, on_device(): pl.pallas_call(kernel, out_shape=(jax.ShapeDtypeStruct((64, depth), bf),...  259 us

profile of v3, /device:TPU:0, one launch (start us, length us, event | category | flops | bytes accessed | tf_op | source)
XLA Modules:
  0.0 264.2 jit_solution(17415736285836634185)
XLA Ops:
  0.6 259.2 %routed_experts.1 = (bf16[64,7168]{1,0:T(8,128)(2,1)}, bf16[64,7168]{1,0:T(8,128)(2,1)}) custom-call(bf16[64,7168]{1,0:T(8,128)(2,1)} %bitcast.24, bf16[64,7168]{1,0:T(8,128)(2,1)} %bitcast.25, f32[1,7168]{1,0:T(1,128)} %gains.1, bf16[7168,256]{1,0:T(8,128)(2,1)} %bitcast.21, bf16[7168,256]{1,0:T(8,128)(2,1)} %bitcast.22, bf16[256,7168]{1,0:T(8,128)(2,1)} %bitcast.23, ...), custom_call_target="tpu_custom_call" | custom-call | tf_op jit(solution)/shard_map/routed_experts/pallas_call | solution.py:723
  259.9 2.2 copy.17
  262.0 2.2 copy.18

commit v4 on v3

--- a/solution.py
+++ b/solution.py
@@ -9,9 +9,11 @@
 EPSILON = 1e-06
 MESH = pl.DeviceIdType.MESH
 CAP = 20
-EARLY = 4
-RING = 4
+EARLY = 5
+
 CHUNK = 512
+LAG = 2
+RING = LAG + 1
 PARTS = 4
 PIECE = 896
 NT = (((1,), (1,)), ((), ()))
@@ -45,13 +47,14 @@
 
 def kernel(
     fwd_in, bwd_grad, gains, wg, wu, wd, f_routes, f_probs, b_routes, b_probs, bwd_input, stash, target,
-    fwd_out, bwd_out,
+    outs,
     told, meta, scales, scale, raw, dense, packed, rows, w_own, w_peer, wd_own, wd_peer, st, acc, psend, precv, small, hid,
     irecv, ipend, back, back2, pend, pend2, orecv, orecv2, xrecv, grad, gres, pack, comb,
     relay_s, relay_r, gres_s, gres_r, scale_s, scale_r, meta_s, meta_r, o_s, o_r, z_s, z_r, i_s, i_r,
     wt_s, wt_r, wd_s, wd_r, p_s, p_r, sm_s, sm_r, hid_s, hid_r,
     ib_s, ib_r, zz_s, zz_r, zzloc, zb_s, zb_r, ob_s, ob_r, xb_s, xb_r, loc, zloc, zbloc,
 ):
+    fwd_out, bwd_out = outs.at[0], outs.at[1]
     depth = gains.shape[1]
     width = depth // 2
     steps = width // CHUNK
@@ -383,23 +386,36 @@
             acc[k, 0] += mm(block, w_own[k, at_c])
             acc[k, 1] += mm(block, w_peer[k, at_c])
 
+    def send_sums():
+        for h in range(2):
+            for k in range(2):
+                psend[1 + k, classes[h]] = acc[k, 1, classes[h]].astype(jnp.bfloat16)
+                p_copy(1 + k, h).start()
+
     def out_grad(c, carry):
-        at_c = aligned(c * CHUNK, CHUNK, CHUNK)
         wait(w_copies(c))
 
         @pl.when(c + 4 < steps)
         def _():
             start(w_copies(c + 4))
 
-        def total(at_rows):
-            value = mm_t(small[0, 0, at_rows], w_own[0, at_c]) + mm_t(small[1, 0, at_rows], w_own[1, at_c])
-            value += mm_t(small[0, 1, at_rows], w_peer[0, at_c])
-            value += mm_t(small[1, 1, at_rows], w_peer[1, at_c])
-            return value
-
-        rows[0, class_peer, at_c] = total(class_peer).astype(jnp.bfloat16)
-        ib_copy(c).start()
-        ipend[c] = total(class_own)
+        def out_chunk(q, carry):
+            at_c = aligned(q * CHUNK, CHUNK, CHUNK)
+
+            def total(at_rows):
+                value = mm_t(small[0, 0, at_rows], w_own[0, at_c]) + mm_t(small[1, 0, at_rows], w_own[1, at_c])
+                value += mm_t(small[0, 1, at_rows], w_peer[0, at_c])
+                value += mm_t(small[1, 1, at_rows], w_peer[1, at_c])
+                return value
+
+            rows[0, class_peer, at_c] = total(class_peer).astype(jnp.bfloat16)
+            ib_copy(q).start()
+            ipend[q] = total(class_own)
+            return carry
+
+        @pl.when(c <= EARLY)
+        def _():
+            out_chunk(c, 0)
 
         @pl.when(c == EARLY)
         def _():
@@ -415,6 +431,14 @@
         @pl.when(c >= EARLY)
         def _():
             gate_sums(c)
+
+        @pl.when(c == steps - 1)
+        def _():
+            send_sums()
+
+        @pl.when(c > EARLY)
+        def _():
+            out_chunk(c, 0)
 
         return carry
 
@@ -572,11 +596,9 @@
         lax.fori_loop(first, last, one, 0)
 
     lax.fori_loop(0, steps, out_grad, 0)
-    for h in range(2):
-        for k in range(2):
-            psend[1 + k, classes[h]] = acc[k, 1, classes[h]].astype(jnp.bfloat16)
-            p_copy(1 + k, h).start()
-    each(0, 2, add_pair)
+    each(0, 4, add_pair)
+    each(0, 3, combine)
+    add_outer(0)
 
     def gated(h):
         for k in range(2):
@@ -594,10 +616,14 @@
         hid_copy(h).start()
 
     gated(0)
-    each(2, 4, add_pair)
+    add_pair(4)
+    combine(3)
+    add_outer(1)
     gated(1)
     gres_copy.start()
-    each(4, 5, add_pair)
+    add_pair(5)
+    combine(4)
+    add_outer(2)
     hid_copy(0).wait()
 
     def step(t, carry):
@@ -619,18 +645,13 @@
             def _():
                 do_odd(q)
 
-        two_ways(t + 5, 5, add_pair, combine_all)
-
-        @pl.when(t == 0)
-        def _():
-            each(0, 3, combine)
-            add_outer(0)
-
-        two_ways(t + 3, 3, combine, add_outer_all)
-        stage(t + 1, 1, add_outer)
-        stage(t - 1, 0, finish)
-
-        @pl.when(t == steps + 1)
+        two_ways(t + steps - LAG, 6, add_pair, combine_all)
+
+        two_ways(t + steps - 2 * LAG, 5, combine, add_outer_all)
+        stage(t + steps - 3 * LAG, 3, add_outer)
+        stage(t + steps - 4 * LAG, max(0, steps - 4 * LAG), finish)
+
+        @pl.when(t == 4 * LAG - 1)
         def _():
             wait(u_loads)
             gres_copy.wait()
@@ -651,7 +672,7 @@
 
         return carry
 
-    lax.fori_loop(0, 2 * steps + 1, step, 0)
+    lax.fori_loop(0, steps + 4 * LAG, step, 0)
 
 
 def on_device(
@@ -708,7 +729,7 @@
         dma((2, PARTS)), dma((2, PARTS)),
         dma((2, PARTS, 3)), dma((2, PARTS, 3)),
         dma((2, PARTS)), dma((2, PARTS)),
-        dma((2, steps)), dma((2, steps)),
+        dma((2, width // CHUNK)), dma((2, width // CHUNK)),
         dma, dma,
         dma((3, 2)), dma((3, 2)),
         dma((2,)), dma((2,)),
@@ -720,11 +741,11 @@
         dma((two,)), dma((two,)),
         dma((7,)), dma((2, PARTS)), dma((two,)),
     ]
-    fwd_result, bwd_result = pl.pallas_call(
+    outs = pl.pallas_call(
         kernel,
-        out_shape=(jax.ShapeDtypeStruct((64, depth), bf), jax.ShapeDtypeStruct((64, depth), bf)),
+        out_shape=jax.ShapeDtypeStruct((2, 64, depth), bf),
         in_specs=[vmem, hbm, vmem, hbm, hbm, hbm, vmem, vmem, vmem, vmem, hbm, hbm, vmem],
-        out_specs=(vmem, vmem),
+        out_specs=vmem,
         scratch_shapes=scratch,
         compiler_params=pltpu.CompilerParams(
             collective_id=0, has_side_effects=True, vmem_limit_bytes=63 * 1024 * 1024
@@ -734,7 +755,7 @@
         fwd_in[0], bwd_grad[0], gains, gate_weight[0], up_weight[0], down_weight[0],
         fwd_routes[0].T, fwd_probs[0].T, bwd_routes[0].T, bwd_probs[0].T, bwd_input[0], bwd_stash[0], goal,
     )
-    return (fwd_result[None], bwd_result[None])
+    return (outs[0:1], outs[1:2])
 
 
 def solution(mesh):

time: 264 us -> 259 us (0.981)
  Pallas kernels: 259 us -> 256 us
    unnamed x2 -> x0, local copies, waits for them, and re-layouts: 4.32 us -> none
    pallas_call x1, Pallas kernels: 259 us -> 256 us  [on_device(): pl.pallas_call(kernel, out_shape=jax.ShapeDtypeStruct((2, 64, depth), bf)...]
    slice x0 -> x1, local copies, waits for them, and re-layouts: none -> 2.8 us  [on_device(): return (outs[0:1], outs[1:2])]
where the time goes in v4:
time: 259 us
  Pallas kernels  256 us (99%)
  local copies, waits for them, and re-layouts  2.8 us (1%)
    pallas_call x1, Pallas kernels, on_device(): pl.pallas_call(kernel, out_shape=jax.ShapeDtypeStruct((2, 64, depth), bf)...  256 us

profile of v4, /device:TPU:0, one launch (start us, length us, event | category | flops | bytes accessed | tf_op | source)
XLA Modules:
  0.0 259.2 jit_solution(16185911663237745287)
XLA Ops:
  0.6 255.8 %routed_experts.1 = bf16[2,64,7168]{2,1,0:T(8,128)(2,1)} custom-call(bf16[64,7168]{1,0:T(8,128)(2,1)} %bitcast.22, bf16[64,7168]{1,0:T(8,128)(2,1)} %bitcast.23, f32[1,7168]{1,0:T(1,128)} %gains.1, bf16[7168,256]{1,0:T(8,128)(2,1)} %bitcast.19, bf16[7168,256]{1,0:T(8,128)(2,1)} %bitcast.20, bf16[256,7168]{1,0:T(8,128)(2,1)} %bitcast.21, s32[2,64]{1,0:T(2,128)} %bitcast.26, ...), custom_call_target="tpu_custom_call" | custom-call | tf_op jit(solution)/shard_map/routed_experts/pallas_call | solution.py:744
  256.4 2.8 %fusion = (bf16[1,64,7168]{2,1,0:T(8,128)(2,1)}, bf16[1,64,7168]{2,1,0:T(8,128)(2,1)}) fusion(bf16[2,64,7168]{2,1,0:T(8,128)(2,1)} %routed_experts.1), kind=kLoop, calls=%fused_computation | loop fusion | bytes 3670016 | tf_op jit(solution)/shard_map/slice | solution.py:758

commit v5 on v4

--- a/solution.py
+++ b/solution.py
@@ -286,7 +286,8 @@
     for c, pair in enumerate(((0, 3), (1, 2))):
         for zz in range(4):
             for k in range(2):
-                blocks = [small[k, 0, zz * 160 + yy * 40 : zz * 160 + yy * 40 + 40].astype(jnp.float32) for yy in pair]
+                wide = small[k, 0, zz * 160 : zz * 160 + 160].astype(jnp.float32)
+                blocks = [wide[yy * 40 : yy * 40 + 40] for yy in pair]
                 at_block = pl.ds(c * 320 + zz * 80, 80)
                 st[at_block, k * hidden : (k + 1) * hidden] = jnp.concatenate(blocks, axis=0).astype(jnp.bfloat16)
     u_loads = [

time: 259 us -> 259 us (level)
  no operation moved by 1% of the time
where the time goes in v5:
time: 259 us
  Pallas kernels  256 us (99%)
  local copies, waits for them, and re-layouts  2.8 us (1%)
    pallas_call x1, Pallas kernels, on_device(): pl.pallas_call(kernel, out_shape=jax.ShapeDtypeStruct((2, 64, depth), bf)...  256 us

profile of v5, /device:TPU:0, one launch (start us, length us, event | category | flops | bytes accessed | tf_op | source)
XLA Modules:
  0.0 259.2 jit_solution(16185911663237745287)
XLA Ops:
  0.6 255.8 %routed_experts.1 = bf16[2,64,7168]{2,1,0:T(8,128)(2,1)} custom-call(bf16[64,7168]{1,0:T(8,128)(2,1)} %bitcast.22, bf16[64,7168]{1,0:T(8,128)(2,1)} %bitcast.23, f32[1,7168]{1,0:T(1,128)} %gains.1, bf16[7168,256]{1,0:T(8,128)(2,1)} %bitcast.19, bf16[7168,256]{1,0:T(8,128)(2,1)} %bitcast.20, bf16[256,7168]{1,0:T(8,128)(2,1)} %bitcast.21, s32[2,64]{1,0:T(2,128)} %bitcast.26, ...), custom_call_target="tpu_custom_call" | custom-call | tf_op jit(solution)/shard_map/routed_experts/pallas_call | solution.py:745
  256.4 2.8 %fusion = (bf16[1,64,7168]{2,1,0:T(8,128)(2,1)}, bf16[1,64,7168]{2,1,0:T(8,128)(2,1)}) fusion(bf16[2,64,7168]{2,1,0:T(8,128)(2,1)} %routed_experts.1), kind=kLoop, calls=%fused_computation | loop fusion | bytes 3670016 | tf_op jit(solution)/shard_map/slice | solution.py:759
